TPU v7x, 128 devices: a whole 4x4x4 slice. The times are simulated.
128 devices in a mesh: row: 8 (over y, z_hi), col: 16 (over x, z_lo, core).
Axes of the slice: x: 4, y: 4, z: 4 (z_hi: 2, z_lo: 2; z = z_hi * 2 + z_lo), core: 2. Of those that a mesh axis runs over, the one named last changes fastest.
Arguments:
- samples: bfloat16 [8192, 8192], P('col'), may hold values from -6 to 6
- shrink: float32 [8192], replicated, may hold values from 0.5 to 2
Outputs:
- factored: float32 [8, 1024, 16, 512], P('row', None, 'col')
All inputs are finite; a program needn't handle non-finite values.
Results may differ from a plain program's by a relative error of at most 0.0003.
Values may be sent and summed in bfloat16 or wider, within the bound.
No kernel may reach another device: no remote copies, remote signals or barrier semaphores. Data moves between devices by JAX's collectives and lax.ppermute only.
A program may use at most 128 MiB of HBM per device.

v0:
```python
import jax
import jax.numpy as jnp
from jax import lax
from jax.sharding import PartitionSpec as P

COL_BLOCK = 256
PANEL = 512


def broadcast(value, axis, source):
    kept = jnp.where(lax.axis_index(axis) == source, value, 0).astype(value.dtype)
    return lax.psum(kept, axis)


def contract_rows(first, second):
    return lax.dot_general(
        first, second, (((0,), (0,)), ((), ())), preferred_element_type=jnp.float32
    )


def body(samples, shrink):
    row_devs = lax.axis_size("row")
    col_devs = lax.axis_size("col")
    row_index = lax.axis_index("row")
    col_index = lax.axis_index("col")
    local_rows, variables = samples.shape
    band_rows = variables // row_devs
    strip_cols = variables // col_devs
    row_block = PANEL // row_devs
    row_groups = band_rows // row_block
    col_groups = strip_cols // COL_BLOCK
    total_rows = local_rows * col_devs
    col_order = (
        samples.reshape(local_rows, col_groups, col_devs, COL_BLOCK)
        .transpose(0, 2, 1, 3)
        .reshape(local_rows, variables)
    )
    own_rows = lax.dynamic_slice_in_dim(samples, row_index * band_rows, band_rows, 1)
    summed = lax.psum_scatter(
        contract_rows(col_order, own_rows), "col", scatter_dimension=0, tiled=True
    )
    block_tile = summed.T
    halves = row_groups // row_devs
    sectioned = block_tile.reshape(1, halves, row_devs, row_block, strip_cols)
    moved = lax.all_to_all(sectioned, "row", split_axis=2, concat_axis=0, tiled=True)
    block_tile = moved.reshape(band_rows, strip_cols)
    row_iota = jnp.arange(band_rows, dtype=jnp.int32)
    col_iota = jnp.arange(strip_cols, dtype=jnp.int32)
    global_row = (row_index + row_devs * (row_iota // row_block)) * row_block + row_iota % row_block
    global_col = (col_index + col_devs * (col_iota // COL_BLOCK)) * COL_BLOCK + col_iota % COL_BLOCK
    shrink_local = lax.dynamic_index_in_dim(
        shrink.reshape(col_groups, col_devs, COL_BLOCK), col_index, 1, False
    ).reshape(strip_cols)
    on_diagonal = global_row[:, None] == global_col[None, :]
    covariance = block_tile / jnp.float32(total_rows) + jnp.where(
        on_diagonal, shrink_local[None, :], jnp.float32(0.0)
    )
    panel_pieces = []
    for root in range(PANEL // COL_BLOCK):
        panel_pieces.append(broadcast(covariance[:, :COL_BLOCK], "col", root))
    panel_rows = jnp.concatenate(panel_pieces, axis=1)
    leading_block, upper_rows = (
        lax.all_gather(panel_rows[:row_block], "row", axis=0, tiled=True),
        lax.all_gather(covariance[:row_block], "row", axis=0, tiled=True),
    )
    leading = jnp.linalg.cholesky(leading_block)
    panel_factor = lax.linalg.triangular_solve(leading, panel_rows.T, left_side=True, lower=True).T
    upper_solve = lax.linalg.triangular_solve(leading, upper_rows, left_side=True, lower=True)
    updated = covariance - jnp.dot(
        panel_factor,
        upper_solve,
        precision=lax.Precision.HIGHEST,
        preferred_element_type=jnp.float32,
    )
    panel_count = PANEL // COL_BLOCK
    chosen = lax.dynamic_slice_in_dim(
        panel_factor, jnp.minimum(col_index, panel_count - 1) * COL_BLOCK, COL_BLOCK, 1
    )
    leading_cols = jnp.where(col_index < panel_count, chosen, updated[:, :COL_BLOCK])
    result = jnp.concatenate([leading_cols, updated[:, COL_BLOCK:]], axis=1)
    return result.reshape(1, band_rows, 1, strip_cols)


def solution(mesh):
    return jax.shard_map(
        body,
        mesh=mesh,
        in_specs=(P("col", None), P()),
        out_specs=P("row", None, "col", None),
        check_vma=False,
    )
```

profile of v0, /device:TPU:1, one launch (start us, length us, event | category | flops | bytes accessed | tf_op | source)
XLA Modules:
  0.0 785.7 jit_solution(18420207621196639818)
XLA Ops:
  6.5 12.0 %copy.19 = bf16[512,8192]{0,1:T(8,128)(2,1)} copy(bf16[512,8192]{1,0:T(8,128)(2,1)} %param.2) | data formatting | bytes 16777216 | tf_op args[0]
  18.5 7.5 copy.20
  26.0 17.8 %convolution_bitcast_fusion = f32[8192,1024]{0,1:T(8,128)} fusion(bf16[512,8192]{0,1:T(8,128)(2,1)} %bitcast.80, bf16[512,8192]{1,0:T(8,128)(2,1)} %param.2, s32[]{:T(128)S(6)} %select_n.81), kind=kOutput, calls=%fused_computation.2 | convolution fusion | flops 8589934592 | bytes 42991620 | tf_op jit(solution)/shard_map/dot_general | solution.py:16
  43.8 352.7 %reduce-scatter.2.cloned.1.call-done = f32[512,1024]{0,1:T(8,128)} async-done(((f32[8192,1024]{0,1:T(8,128)}), f32[512,1024]{0,1:T(8,128)}) %reduce-scatter.2.cloned.1.call-update) | async-done | bytes 2097168 | tf_op jit(solution)/shard_map/reduce_scatter | solution.py:39
  396.5 3.1 copy.21
  399.7 6.4 all-to-all-start
  406.2 27.2 %all-to-all-done = f32[1,2,8,64,512]{4,3,1,0,2:T(8,128)S(1)} async-done(((f32[1,2,8,64,512]{4,3,1,0,2:T(8,128)}), f32[1,2,8,64,512]{4,3,1,0,2:T(8,128)S(1)}, u32[]{:S(2)}, u32[]{:S(2)}) %all-to-all-start) | async-done | bytes 2097184 | tf_op jit(solution)/shard_map/all_to_all | solution.py:45
  433.4 1.6 bitcast_multiply_fusion
  435.0 2.9 copy.23
  437.9 1.9 select_add_fusion
  439.8 1.7 slice_select_fusion.1
  441.5 118.2 %all-reduce.4.cloned.1.call-done = (f32[1024,256]{0,1:T(8,128)}, f32[1024,256]{0,1:T(8,128)}) async-done(((f32[1024,256]{0,1:T(8,128)}, f32[1024,256]{0,1:T(8,128)}), (f32[1024,256]{0,1:T(8,128)}, f32[1024,256]{0,1:T(8,128)})) %all-reduce.4.cloned.1.call-update) | async-done | bytes 2097168 | tf_op jit(solution)/shard_map/psum | solution.py:12
  559.7 1.4 constant_dynamic-update-slice_fusion.1
  561.4 1.3 copy-done
  562.7 0.8 copy.24
  563.8 0.8 copy.26
  564.6 46.7 %all-gather.3.cloned.1.call-done = f32[512,512]{1,0:T(8,128)} async-done(((f32[64,512]{1,0:T(8,128)}), f32[512,512]{1,0:T(8,128)}) %all-gather.3.cloned.1.call-update) | async-done | bytes 1048592 | tf_op jit(solution)/shard_map/all_gather | solution.py:63
  611.3 2.6 copy.25
  614.0 1.4 fusion.19
  615.5 1.0 copy-done.4
  616.5 11.7 %cholesky.104 = f32[128,128]{1,0:T(8,128)S(1)} custom-call(f32[128,128]{1,0:T(8,128)S(1)} %cholesky.266), custom_call_target="Cholesky" | custom-call | tf_op jit(solution)/shard_map/jit(cholesky)/cholesky | solution.py:66
  628.4 9.8 %custom-call.32 = f32[1,128,128]{1,2,0:T(8,128)S(1)} custom-call(f32[1,128,128]{2,1,0:T(8,128)S(1)} %get-tuple-element.38), custom_call_target="InvertDiagBlocksLowerTriangular" | custom-call | tf_op jit(solution)/shard_map/jit(cholesky)/cholesky | solution.py:66
  638.2 1.2 constant_dynamic-update-slice_fusion.2
  639.4 1.3 convolution_subtract_fusion.6
  640.7 11.7 %cholesky.217 = f32[128,128]{1,0:T(8,128)S(1)} custom-call(f32[128,128]{1,0:T(8,128)S(1)} %cholesky.270), custom_call_target="Cholesky" | custom-call | tf_op jit(solution)/shard_map/jit(cholesky)/cholesky | solution.py:66
  652.4 10.2 %custom-call.33 = f32[1,128,128]{1,2,0:T(8,128)S(1)} custom-call(f32[1,128,128]{2,1,0:T(8,128)S(1)} %get-tuple-element.35), custom_call_target="InvertDiagBlocksLowerTriangular" | custom-call | tf_op jit(solution)/shard_map/jit(cholesky)/cholesky | solution.py:66
  662.9 1.3 convolution_subtract_fusion.7
  664.2 11.7 %cholesky.238 = f32[128,128]{1,0:T(8,128)S(1)} custom-call(f32[128,128]{1,0:T(8,128)S(1)} %cholesky.275), custom_call_target="Cholesky" | custom-call | tf_op jit(solution)/shard_map/jit(cholesky)/cholesky | solution.py:66
  675.9 9.8 %custom-call.34 = f32[1,128,128]{1,2,0:T(8,128)S(1)} custom-call(f32[1,128,128]{2,1,0:T(8,128)S(1)} %get-tuple-element.32), custom_call_target="InvertDiagBlocksLowerTriangular" | custom-call | tf_op jit(solution)/shard_map/jit(cholesky)/cholesky | solution.py:66
  686.0 1.2 convolution_subtract_fusion.8
  687.2 11.7 %cholesky.255 = f32[128,128]{1,0:T(8,128)S(1)} custom-call(f32[128,128]{1,0:T(8,128)S(1)} %convolution_subtract_fusion.8), custom_call_target="Cholesky" | custom-call | tf_op jit(solution)/shard_map/jit(cholesky)/cholesky | solution.py:66
  699.0 0.7 compare_reduce_fusion.2
  700.9 0.8 compare_reduce_fusion.1
  703.4 1.1 select_select_fusion
  704.6 14.0 %while.1 = (s32[]{:T(128)}, f32[512,512]{1,0:T(8,128)}, s32[4,2]{0,1:T(2,128)S(1)}, f32[4,128,128]{2,1,0:T(8,128)}, s32[]{:T(128)}) while((s32[]{:T(128)}, f32[512,512]{1,0:T(8,128)}, s32[4,2]{0,1:T(2,128)S(1)}, f32[4,128,128]{2,1,0:T(8,128)}, s32[]{:T(128)}) %tuple.29), condition=%wide.while_cond, body=%wide.while_body.sunk | while | flops 2 | bytes 132205 | solution.py:67
  705.2 2.9 bitcast_dynamic-update-slice_fusion.2
  708.7 2.9 bitcast_dynamic-update-slice_fusion.2
  712.3 2.9 bitcast_dynamic-update-slice_fusion.2
  715.8 2.8 bitcast_dynamic-update-slice_fusion.2
  718.6 40.2 %custom-call.35 = f32[4,128,128]{1,2,0:T(8,128)S(1)} custom-call(f32[4,128,128]{2,1,0:T(8,128)} %get-tuple-element.12), custom_call_target="InvertDiagBlocksLowerTriangular" | custom-call | tf_op jit(solution)/shard_map/triangular_solve | solution.py:67
  758.8 1.4 fusion.31
  760.2 1.4 convolution_subtract_fusion.4
  762.0 1.6 convolution_subtract_fusion.3
  764.0 1.6 convolution_subtract_fusion.5
  767.9 0.7 convolution_subtract_fusion.1
  769.3 1.1 fusion.6
  771.3 3.6 convolution_subtract_fusion
  775.3 3.7 copy.27
  (61 shorter events, 9.7 us)
Async XLA Ops:
  6.5 390.0 %reduce-scatter.2.cloned.1.call-start = ((), (), s32[]{:S(2)}) async-start(), calls=%async_computation.2 | async-start | bytes 35651584 | tf_op jit(solution)/shard_map/reduce_scatter | solution.py:39
  399.7 6.5 copy-start.6
  399.7 33.7 %all-to-all-start = ((f32[1,2,8,64,512]{4,3,1,0,2:T(8,128)}), f32[1,2,8,64,512]{4,3,1,0,2:T(8,128)S(1)}, u32[]{:S(2)}, u32[]{:S(2)}) async-start(f32[1,2,8,64,512]{4,3,1,0,2:T(8,128)} %copy.21), calls=%async_computation.1 | async-start | bytes 4194304 | tf_op jit(solution)/shard_map/all_to_all | solution.py:45
  406.1 153.6 %all-reduce.4.cloned.1.call-start = ((), (), s32[]{:S(2)}) async-start(), calls=%async_computation.5 | async-start | bytes 4194304 | tf_op jit(solution)/shard_map/psum | solution.py:12
  441.5 169.9 %all-gather.3.cloned.1.call-start = ((), (), s32[]{:S(2)}) async-start(), calls=%async_computation.3 | async-start | bytes 1179648 | tf_op jit(solution)/shard_map/all_gather | solution.py:63
  559.7 1.5 copy-start.5
  561.4 1.3 copy-start
  563.5 195.3 %all-gather.5.cloned.1.call-start = ((), (), s32[]{:S(2)}) async-start(), calls=%async_computation.4 | async-start | bytes 1179648 | tf_op jit(solution)/shard_map/all_gather | solution.py:64
  611.3 2.7 copy-start.3
  615.4 1.0 copy-start.4
  718.6 43.4 %copy-start.2 = (f32[512,512]{1,0:T(8,128)S(1)}, f32[512,512]{1,0:T(8,128)}, u32[]{:S(2)}) copy-start(f32[512,512]{1,0:T(8,128)} %get-tuple-element.99) | copy-start | bytes 3145732
  761.6 4.5 copy-start.1
Sparse Core Ops, SparseCore 0:
  43.9 352.5 reduce-scatter.1
  441.6 118.0 all-reduce.3
  563.6 47.6 all-gather.2
  613.5 45.8 all-gather.4
where the time goes:
time: 792 us; the launch traced here: 786 us
  waiting for transfers between devices  545 us (69%)
  other arithmetic  127 us (16%)
  local copies, waits for them, and re-layouts  51.6 us (7%)
  matrix products  39 us (5%)
  between operations  16.1 us (2%)
    reduce_scatter x1, waiting for transfers between devices, body(): lax.psum_scatter(contract_rows(col_order, own_rows), 'col', scatter_dimen...  353 us
    psum x1, waiting for transfers between devices, broadcast(): return lax.psum(kept, axis)  118 us
    another operation x14, other arithmetic, body(): leading = jnp.linalg.cholesky(leading_block)  78.9 us
    all_gather x1, waiting for transfers between devices, body(): lax.all_gather(panel_rows[:row_block], 'row', axis=0, tiled=True)  46.7 us
    another operation x4, other arithmetic, body(): lax.linalg.triangular_solve(leading, panel_rows.T, left_side=True, lower=...  41.6 us
    all_to_all x1, waiting for transfers between devices, body(): lax.all_to_all(sectioned, 'row', split_axis=2, concat_axis=0, tiled=True)  27.2 us
    dot_general x1, matrix products, contract_rows(): lax.dot_general(first, second, (((0,), (0,)), ((), ())), preferred_elemen...  17.8 us
    unnamed x16, local copies, waits for them, and re-layouts  15.9 us
  transfers between devices with their start and end apart: 5, of which 4 were waited for; matrix products, arithmetic and copies ran while one was open for 18% of the time, Pallas kernels for 0%

commit v1 on v0

v1 whole, which is shorter than its diff:
```python
import jax
import jax.numpy as jnp
from jax import lax
from jax.experimental import pallas as pl
from jax.experimental.pallas import tpu as pltpu
from jax.sharding import Mesh, PartitionSpec as P

PANEL = 512
VARS = 8192
ROWS = 512
HI = lax.Precision.HIGHEST
F32 = jnp.float32
BF = jnp.bfloat16
MB = 1 << 20


def cost(us):
    return pl.CostEstimate(flops=us << 30, bytes_accessed=1 << 16, transcendentals=0)


ANY = pl.BlockSpec(memory_space=pl.ANY)
VM = pl.BlockSpec(memory_space=pltpu.VMEM)


def params(mb):
    return pltpu.CompilerParams(vmem_limit_bytes=mb * MB)


def nt(a, b, precision=None):
    return lax.dot_general(
        a, b, (((1,), (1,)), ((), ())), precision=precision, preferred_element_type=F32
    )


def nn(a, b, precision=None):
    return lax.dot_general(
        a, b, (((1,), (0,)), ((), ())), precision=precision, preferred_element_type=F32
    )


def prep_kernel(lo_ref, hi_ref, rows_ref, up_ref, down_ref, lead_ref, strip_ref, pick_ref):
    y, zh, zl = lax.axis_index("y"), lax.axis_index("zh"), lax.axis_index("zl")
    r = y * 2 + zh
    core = lax.axis_index("core")
    @pl.when(pl.program_id(0) == 0)
    def _():
        j = lax.broadcasted_iota(jnp.int32, (512, 128), 0)
        i = lax.broadcasted_iota(jnp.int32, (512, 128), 1)
        for h, by in enumerate((1, 3)):
            other = y * 2 + lax.rem(zh * 2 + zl + by, 4) // 2
            want = jnp.where(i < 64, r * 64 + i, other * 64 + i - 64)
            pick_ref[h] = jnp.where(j == want, 1.0, 0.0).astype(BF)

    mine = pl.ds(pl.multiple_of((zh * 4 + y) * 64, 64), 64)
    for h, (ref, out) in enumerate(((lo_ref, up_ref), (hi_ref, down_ref))):
        picked = nn(ref[...], pick_ref[h]).astype(BF).T
        rows_ref[h, 0] = picked[:64]
        out[0] = picked[64:]
        part = ref[mine, :]
        left, right = part[:, :256], part[:, 256:]
        strip_ref[0, :, h * 256 : h * 256 + 256] = jnp.where(core == 0, left, right)
        strip_ref[0, :, 512 + h * 256 : 768 + h * 256] = jnp.where(core == 0, right, left)

    @pl.when(pl.program_id(0) == 0)
    def _():
        lead_ref[...] = lo_ref[...].T


def prep(x):
    rows, up, down, lead, strip = pl.pallas_call(
        prep_kernel,
        grid=(8,),
        in_specs=[
            pl.BlockSpec((ROWS, 512), lambda k: (0, k)),
            pl.BlockSpec((ROWS, 512), lambda k: (0, k + 8)),
        ],
        out_specs=[
            pl.BlockSpec((2, 1, 64, ROWS), lambda k: (0, k, 0, 0)),
            pl.BlockSpec((1, 64, ROWS), lambda k: (k, 0, 0)),
            pl.BlockSpec((1, 64, ROWS), lambda k: (k, 0, 0)),
            pl.BlockSpec((512, ROWS), lambda k: (0, 0)),
            pl.BlockSpec((1, 64, 1024), lambda k: (k, 0, 0)),
        ],
        out_shape=[
            jax.ShapeDtypeStruct((2, 8, 64, ROWS), BF),
            jax.ShapeDtypeStruct((8, 64, ROWS), BF),
            jax.ShapeDtypeStruct((8, 64, ROWS), BF),
            jax.ShapeDtypeStruct((512, ROWS), BF),
            jax.ShapeDtypeStruct((8, 64, 1024), BF),
        ],
        scratch_shapes=[pltpu.VMEM((2, 512, 128), BF)],
        compiler_params=params(58),
        cost_estimate=cost(9),
        name="prep",
    )(x, x)
    return rows.reshape(1024, ROWS), up.reshape(512, ROWS), down.reshape(512, ROWS), lead, strip


def place(dx, dz):
    return lax.rem(lax.axis_index("x") + dx, 4) * 2 + lax.rem(lax.axis_index("zl") + dz, 2)


def lead_kernel(*refs):
    gram_ref, all_ref = refs[-2:]
    for dz in range(2):
        for n, dx in enumerate((0, 1, 3, 2)):
            all_ref[place(dx, dz)] = refs[4 * dz + n][...]
    total = None
    for k in range(8):
        v = all_ref[k]
        term = nt(v, v)
        total = term if total is None else total + term
    gram_ref[...] = total


def lead_gram(pieces):
    return pl.pallas_call(
        lead_kernel,
        in_specs=[VM] * len(pieces),
        out_specs=[VM, VM],
        out_shape=[
            jax.ShapeDtypeStruct((512, 512), F32),
            jax.ShapeDtypeStruct((8, 512, 512), BF),
        ],
        compiler_params=params(24),
        cost_estimate=cost(4),
        name="lead_gram",
    )(*pieces)


def factor128(block):
    tiles = [block[8 * t : 8 * t + 8, :] for t in range(16)]
    lane = lax.broadcasted_iota(jnp.int32, (8, 128), 1)
    sub = lax.broadcasted_iota(jnp.int32, (8, 128), 0)
    out = []
    for g in range(16):
        j0 = 8 * g
        group = (lane >= j0) & (lane < j0 + 8)
        cols = [jnp.broadcast_to(tiles[g][:, j0 + s : j0 + s + 1], (8, 128)) for s in range(8)]
        jordan = jnp.where(group, jnp.where(lane - j0 == sub, 1.0, 0.0), tiles[g])
        kept = jnp.zeros((8, 128), F32)
        invs = jnp.ones((8, 128), F32)
        for s in range(8):
            here = sub == s
            inv = 1.0 / jnp.broadcast_to(cols[s][s : s + 1, :], (8, 128))
            row = jnp.broadcast_to(jordan[s : s + 1, :], (8, 128))
            kept = jnp.where(here, row, kept)
            invs = jnp.where(here, inv, invs)
            factor = jnp.where(here, 1.0 - inv, cols[s] * inv)
            jordan = jordan - factor * row
            for q in range(s + 1, 8):
                cols[q] = cols[q] - factor * jnp.broadcast_to(cols[q][s : s + 1, :], (8, 128))
        out.append(jnp.where(lane <= sub + j0, kept * jnp.sqrt(invs), 0.0))
        for t in range(g + 1, 16):
            tile = jnp.where(group, 0.0, tiles[t])
            for s in range(8):
                tile = tile - tiles[t][:, j0 + s : j0 + s + 1] * jordan[s : s + 1, :]
            tiles[t] = tile
    return jnp.concatenate(out, axis=0)


def chol_blocks(a_ref, inv_ref, blocks):
    for b in blocks:
        lo, hi = b * 128, b * 128 + 128
        w = factor128(a_ref[lo:hi, lo:hi])
        if b > 0:
            mid = nn(a_ref[lo:hi, :lo], inv_ref[:lo, :lo], HI)
            inv_ref[lo:hi, :lo] = -nn(w, mid, HI)
        inv_ref[lo:hi, lo:hi] = w
        if b < 3:
            below = nt(a_ref[hi:, lo:hi], w, HI)
            a_ref[hi:, lo:hi] = below
            a_ref[hi:, hi:] = a_ref[hi:, hi:] - nt(below, below, HI)


def chol_first(g0, g1, shrink_ref, a_ref, inv_ref):
    i = lax.broadcasted_iota(jnp.int32, (512, 512), 0)
    j = lax.broadcasted_iota(jnp.int32, (512, 512), 1)
    a_ref[...] = (g0[...] + g1[...]) * F32(1.0 / VARS) + jnp.where(
        i == j, shrink_ref[...], 0.0
    )
    inv_ref[...] = jnp.zeros((512, 512), F32)
    chol_blocks(a_ref, inv_ref, (0, 1))


def chol_second(a0, i0, inv_ref, a_ref):
    a_ref[...] = a0[...]
    inv_ref[...] = i0[...]
    chol_blocks(a_ref, inv_ref, (2, 3))


SQUARE = jax.ShapeDtypeStruct((512, 512), F32)


def chol_half(g0, g1, shrink_lead):
    return pl.pallas_call(
        chol_first,
        in_specs=[VM] * 3,
        out_specs=[VM, VM],
        out_shape=[SQUARE, SQUARE],
        compiler_params=params(16),
        cost_estimate=cost(80),
        name="chol_first",
    )(g0, g1, shrink_lead)


def chol_rest(a, inv):
    return pl.pallas_call(
        chol_second,
        in_specs=[VM, VM],
        out_specs=VM,
        out_shape=SQUARE,
        scratch_shapes=[pltpu.VMEM((512, 512), F32)],
        compiler_params=params(16),
        cost_estimate=cost(80),
        name="chol_second",
    )(a, inv)


TALL = jax.ShapeDtypeStruct((1024, 512), F32)
ORDER = tuple((dx, dz) for dz in range(2) for dx in (0, 1, 3, 2))


def fetch(b_ref, b_s, sems):
    copies = []
    for y in range(4):
        c = pltpu.make_async_copy(b_ref.at[y], b_s.at[:, y], sems.at[y])
        c.start()
        copies.append(c)
    for c in copies:
        c.wait()


def half_lanes(dz):
    zh = lax.rem(lax.axis_index("zh") + dz, 2)
    return pl.ds(pl.multiple_of(zh * 256, 256), 256)


def lead_products(l_ref, b_s, lanes, m):
    rows = pl.ds(pl.multiple_of(m * 256, 256), 256)
    total = None
    for k in range(8):
        term = nn(l_ref[k, rows, lanes], b_s[k].reshape(256, 1024))
        total = term if total is None else total + term
    return rows, total


def row_products(a_in, b_s, lanes):
    total = None
    for ref, (dx, dz) in zip(a_in, ORDER):
        term = nn(ref[:, lanes], b_s[place(dx, dz)].reshape(256, 1024))
        total = term if total is None else total + term
    return total


def first_kernel(*refs):
    a_in, l_ref, b_ref = refs[:8], refs[8], refs[9]
    own, other, rl, lc_own, lc_other, b_s, sems = refs[10:]
    lanes = half_lanes(0)

    @pl.when(pl.program_id(0) == 0)
    def _():
        fetch(b_ref, b_s, sems)

        def step(m, _):
            rows, total = lead_products(l_ref, b_s, lanes, m)
            lc_own[rows, :] = total[:, :512]
            lc_other[rows, :] = total[:, 512:]
            return 0

        lax.fori_loop(0, 2, step, 0)

    tile = row_products(a_in, b_s, lanes)
    own[...] = tile[:, :512]
    other[...] = tile[:, 512:]
    side = None
    for ref, (dx, dz) in zip(a_in, ORDER):
        term = nt(ref[...], l_ref[place(dx, dz)])
        side = term if side is None else side + term
    rl[...] = side


def second_kernel(*refs):
    a_in, l_ref, b_ref = refs[:8], refs[8], refs[9]
    own0, other0, lc_own0, lc_other0 = refs[10:14]
    own, other, lc_own, lc_other, b_s, sems = refs[15:]
    lanes = half_lanes(1)

    @pl.when(pl.program_id(0) == 0)
    def _():
        fetch(b_ref, b_s, sems)

        def step(m, _):
            rows, total = lead_products(l_ref, b_s, lanes, m)
            lc_own[rows, :] = lc_own0[rows, :] + total[:, :512]
            lc_other[rows, :] = lc_other0[rows, :] + total[:, 512:]
            return 0

        lax.fori_loop(0, 2, step, 0)

    tile = row_products(a_in, b_s, lanes)
    own[...] = own0[...] + tile[:, :512]
    other[...] = other0[...] + tile[:, 512:]


def once(*shape):
    return pl.BlockSpec(shape, lambda m: (0,) * len(shape))


BLOCK = pl.BlockSpec((256, 512), lambda m: (m, 0))
SCRATCH = [pltpu.VMEM((8, 4, 64, 1024), BF), pltpu.SemaphoreType.DMA((4,))]


def gram_first(a, lead, b):
    return pl.pallas_call(
        first_kernel,
        grid=(4,),
        in_specs=[BLOCK] * 8 + [once(8, 512, 512), ANY],
        out_specs=[BLOCK] * 3 + [once(512, 512)] * 2,
        out_shape=[TALL] * 3 + [SQUARE] * 2,
        scratch_shapes=SCRATCH,
        compiler_params=params(40),
        cost_estimate=cost(17),
        name="gram_first",
    )(*a, lead, b)


def gram_second(a, lead, b, own, other, lc_own, lc_other, after):
    return pl.pallas_call(
        second_kernel,
        grid=(4,),
        in_specs=[BLOCK] * 8
        + [once(8, 512, 512), ANY]
        + [BLOCK] * 2
        + [once(512, 512)] * 2
        + [ANY],
        out_specs=[BLOCK] * 2 + [once(512, 512)] * 2,
        out_shape=[TALL] * 2 + [SQUARE] * 2,
        scratch_shapes=SCRATCH,
        compiler_params=params(40),
        cost_estimate=cost(10),
        name="gram_second",
    )(*a, lead, b, own, other, lc_own, lc_other, after)


def column_of(lane):
    k = lax.axis_index("x") * 2 + lax.axis_index("zl")
    return (lane // 256) * 4096 + k * 512 + lax.axis_index("core") * 256 + lane % 256


def row_of(step):
    r = lax.axis_index("y") * 2 + lax.axis_index("zh")
    local = lax.broadcasted_iota(jnp.int32, (256, 512), 0) + step * 256
    return (local // 64) * 512 + r * 64 + local % 64


def panel_kernel(rm, rr, inv_ref, sl_ref, p_ref):
    lane = lax.broadcasted_iota(jnp.int32, (256, 512), 1)
    c = (rm[...] + rr[...]) * F32(1.0 / VARS) + jnp.where(
        row_of(pl.program_id(0)) == lane, sl_ref[...], 0.0
    )
    p_ref[...] = nt(c, inv_ref[...], HI)


def panel(rm, rr, inv, sl):
    return pl.pallas_call(
        panel_kernel,
        grid=(4,),
        in_specs=[BLOCK] * 2 + [once(512, 512), once(1, 512)],
        out_specs=BLOCK,
        out_shape=TALL,
        compiler_params=params(24),
        cost_estimate=cost(5),
        name="panel",
    )(rm, rr, inv, sl)


def final_kernel(tm, tr, p_ref, lm, lr, inv_ref, sc_ref, out_ref, u_ref):
    k = lax.axis_index("x") * 2 + lax.axis_index("zl")
    core = lax.axis_index("core")
    scale = F32(1.0 / VARS)

    @pl.when(pl.program_id(0) == 0)
    def _():
        row = lax.broadcasted_iota(jnp.int32, (512, 512), 0)
        col = column_of(lax.broadcasted_iota(jnp.int32, (512, 512), 1))
        c = (lm[...] + lr[...]) * scale + jnp.where(row == col, sc_ref[...], 0.0)
        u_ref[...] = nn(inv_ref[...], c, HI)

    p = p_ref[...]
    col = column_of(lax.broadcasted_iota(jnp.int32, (256, 512), 1))
    c = (tm[...] + tr[...]) * scale + jnp.where(
        row_of(pl.program_id(0)) == col, sc_ref[...], 0.0
    )
    out_ref[...] = c - nn(p, u_ref[...], HI)

    @pl.when(k == 0)
    def _():
        out_ref[:, :256] = jnp.where(core == 0, p[:, :256], p[:, 256:])


def final(tm, tr, p, lm, lr, inv, sc):
    return pl.pallas_call(
        final_kernel,
        grid=(4,),
        in_specs=[BLOCK] * 3 + [once(512, 512)] * 3 + [once(1, 512)],
        out_specs=BLOCK,
        out_shape=TALL,
        scratch_shapes=[pltpu.VMEM((512, 512), F32)],
        compiler_params=params(32),
        cost_estimate=cost(9),
        name="final",
    )(tm, tr, p, lm, lr, inv, sc)


def shift(v, axis, by):
    n = lax.axis_size(axis)
    return lax.ppermute(v, axis, [(i, (i + by) % n) for i in range(n)])


def after(v, *others):
    return lax.optimization_barrier((v, *others))[0]


def near(v, axis):
    return shift(v, axis, -1), shift(v, axis, 1)


def body(samples, shrink):
    k = lax.axis_index("x") * 2 + lax.axis_index("zl")
    core = lax.axis_index("core")
    zz = ("zh", "zl")
    rows, up, down, lead, strip = prep(samples)
    cols = lax.all_to_all(strip, ("x", "zl"), split_axis=0, concat_axis=0, tiled=True)

    lead_z = shift(lead, "zl", 1)
    rows_z = jnp.concatenate([shift(up, zz, 1), shift(down, zz, -1)], axis=0)
    l_up, l_down = near(lead, "x")
    lead_z, l_up, l_down, cols = lax.optimization_barrier((lead_z, l_up, l_down, cols))
    lz_up, lz_down = near(lead_z, "x")
    l_far, lz_far = shift(l_down, "x", 1), shift(lz_up, "x", -1)
    cols_z = shift(cols, "zh", 1)
    b_own = lax.all_gather(cols, "y")
    b_z = lax.all_gather(cols_z, "y")
    a_up, a_down = near(rows, "x")
    az_up, az_down = near(rows_z, "x")
    g, lead_all = lead_gram([lead, l_up, l_down, l_far, lead_z, lz_up, lz_down, lz_far])
    sl = shrink[:PANEL].reshape(1, PANEL)
    half_a, half_inv = chol_half(g, shift(g, "core", 1), sl)
    inv = chol_rest(half_a, half_inv)
    a_far, az_far = shift(a_down, "x", 1), shift(az_up, "x", -1)

    a = [rows, a_up, a_down, a_far, rows_z, az_up, az_down, az_far]
    parts = gram_first(a, lead_all, b_own)
    rl = parts[2]
    p = panel(rl, shift(rl, "core", 1), inv, sl)
    own, other, lc_own, lc_other = gram_second(a, lead_all, b_z, *parts[:2], *parts[3:], p)
    sc = lax.dynamic_slice(shrink.reshape(2, 16, 256), (0, 2 * k + core, 0), (2, 1, 256))
    sc = sc.reshape(1, 512)
    out = final(own, shift(other, "core", 1), p, lc_own, shift(lc_other, "core", 1), inv, sc)
    return out.reshape(1, 1024, 1, 512)


def solution(mesh):
    fine = Mesh(mesh.devices.reshape(4, 2, 4, 2, 2), ("y", "zh", "x", "zl", "core"))
    return jax.shard_map(
        body,
        mesh=fine,
        in_specs=(P(("x", "zl", "core"), None), P()),
        out_specs=P(("y", "zh"), None, ("x", "zl", "core"), None),
        check_vma=False,
    )
```

time: 792 us -> 237 us (0.30)
  waiting for transfers between devices: 545 us -> 74.7 us
  other arithmetic: 127 us -> 0 us
  Pallas kernels: 0 us -> 83.1 us
  matrix products: 39 us -> 0 us
  starting transfers between devices: 6.72 us -> 38.9 us
  local copies, waits for them, and re-layouts: 51.6 us -> 26.1 us
    reduce_scatter x1 -> x0, waiting for transfers between devices: 353 us -> none  [body(): lax.psum_scatter(contract_rows(col_order, own_rows), 'col', scatter_dimen...]
    another operation x18 -> x0, other arithmetic: 120 us -> none  [the longest x14 78.9 us: body(): leading = jnp.linalg.cholesky(leading_block)]
    psum x1 -> x0, waiting for transfers between devices: 118 us -> none  [broadcast(): return lax.psum(kept, axis)]
    pallas_call x0 -> x8, Pallas kernels: none -> 83.1 us  [the longest x1 17.8 us: gram_first(): pl.pallas_call(first_kernel, grid=(4,), in_specs=[BLOCK] * 8 + [once(8, 5...]
    ppermute x0 -> x20, waiting for transfers between devices: none -> 74.7 us  [shift(): return lax.ppermute(v, axis, [(i, (i + by) % n) for i in range(n)])]
    all_gather x2, waiting for transfers between devices: 46.8 us -> 0.01 us  [the longest x1 0.01 us: body(): b_own = lax.all_gather(cols, 'y')]
    ppermute x0 -> x20, starting transfers between devices: none -> 32.5 us  [shift(): return lax.ppermute(v, axis, [(i, (i + by) % n) for i in range(n)])]
    all_to_all x1, waiting for transfers between devices: 27.2 us -> 0.01 us  [body(): lax.all_to_all(strip, ('x', 'zl'), split_axis=0, concat_axis=0, tiled=True)]
  transfers between devices with their start and end apart: 5 -> 23, of which waited for: 4 -> 9; matrix products, arithmetic and copies ran while one was open for 18% -> 0% of each run, Pallas kernels for 0% -> 22%
where the time goes in v1:
time: 237 us; the launch traced here: 236 us
  Pallas kernels  83.1 us (35%)
  waiting for transfers between devices  74.7 us (32%)
  starting transfers between devices  38.9 us (16%)
  local copies, waits for them, and re-layouts  26.1 us (11%)
  between operations  13.7 us (6%)
    ppermute x20, waiting for transfers between devices, shift(): return lax.ppermute(v, axis, [(i, (i + by) % n) for i in range(n)])  74.7 us
    ppermute x20, starting transfers between devices, shift(): return lax.ppermute(v, axis, [(i, (i + by) % n) for i in range(n)])  32.5 us
    unnamed x61, local copies, waits for them, and re-layouts  21.9 us
    pallas_call x1, Pallas kernels, gram_first(): pl.pallas_call(first_kernel, grid=(4,), in_specs=[BLOCK] * 8 + [once(8, 5...  17.8 us
    pallas_call x1, Pallas kernels, gram_second(): pl.pallas_call(second_kernel, grid=(4,), in_specs=[BLOCK] * 8 + [once(8,...  14.7 us
    pallas_call x1, Pallas kernels, chol_half(): pl.pallas_call(chol_first, in_specs=[VM] * 3, out_specs=[VM, VM], out_sha...  12.9 us
    pallas_call x1, Pallas kernels, chol_rest(): pl.pallas_call(chol_second, in_specs=[VM, VM], out_specs=VM, out_shape=SQ...  10.6 us
    pallas_call x1, Pallas kernels, prep(): pl.pallas_call(prep_kernel, grid=(8,), in_specs=[pl.BlockSpec((ROWS, 512)...  9.3 us
  transfers between devices with their start and end apart: 23, of which 9 were waited for; matrix products, arithmetic and copies ran while one was open for 0% of the time, Pallas kernels for 22%

profile of v1, /device:TPU:1, one launch (start us, length us, event | category | flops | bytes accessed | tf_op | source)
XLA Modules:
  0.0 236.5 jit_solution(8038759480805650234)
XLA Ops:
  6.5 9.3 %prep.1 = (bf16[2,8,64,512]{3,2,1,0:T(8,128)(2,1)}, bf16[8,64,512]{2,1,0:T(8,128)(2,1)}, bf16[8,64,512]{2,1,0:T(8,128)(2,1)}, bf16[512,512]{1,0:T(8,128)(2,1)}, bf16[8,64,1024]{2,1,0:T(8,128)(2,1)}) custom-call(bf16[512,8192]{1,0:T(8,128)(2,1)} %hi_ref.1, bf16[512,8192]{1,0:T(8,128)(2,1)} %hi_ref.1), custom_call_target="tpu_custom_call" | custom-call | flops 9663676416 | bytes 65536 | tf_op jit(solution)/shard_map/prep/pallas_call | solution.py:70
  15.9 6.4 %all-to-all-start = ((bf16[8,64,1024]{2,1,0:T(8,128)(2,1)}), bf16[8,64,1024]{2,1,0:T(8,128)(2,1)S(1)}, u32[]{:S(2)}, u32[]{:S(2)}) async-start(bf16[8,64,1024]{2,1,0:T(8,128)(2,1)} %get-tuple-element.31), calls=%async_computation | async-start | bytes 2097152 | tf_op jit(solution)/shard_map/all_to_all | solution.py:434
  22.3 1.5 collective-permute-start.10
  23.7 1.2 collective-permute-start.8
  24.9 1.5 collective-permute-start.9
  26.4 21.0 %collective-permute-done.10.refs_2_ = bf16[512,512]{1,0:T(8,128)(2,1)} collective-permute-done((bf16[512,512]{1,0:T(8,128)(2,1)S(1)}, bf16[512,512]{1,0:T(8,128)(2,1)}, u32[]{:S(2)}, u32[]{:S(2)}) %collective-permute-start.10) | collective-permute-done | bytes 524320 | tf_op jit(solution)/shard_map/ppermute | solution.py:418
  48.2 1.0 copy-done.26
  49.3 1.7 collective-permute-start.12
  51.0 0.9 collective-permute-start.3
  52.0 2.1 collective-permute-start.4
  54.1 1.1 collective-permute-start.13
  55.2 5.9 %collective-permute-done.12.refs_5_ = bf16[512,512]{1,0:T(8,128)(2,1)S(1)} collective-permute-done((bf16[512,512]{1,0:T(8,128)(2,1)}, bf16[512,512]{1,0:T(8,128)(2,1)S(1)}, u32[]{:S(2)}, u32[]{:S(2)}) %collective-permute-start.12) | collective-permute-done | bytes 524320 | tf_op jit(solution)/shard_map/ppermute | solution.py:418
  61.2 3.1 %collective-permute-start.14 = (bf16[512,512]{1,0:T(8,128)(2,1)S(1)}, bf16[512,512]{1,0:T(8,128)(2,1)S(1)}, u32[]{:S(2)}, u32[]{:S(2)}) collective-permute-start(bf16[512,512]{1,0:T(8,128)(2,1)S(1)} %collective-permute-done.12.refs_5_), channel_id=1, source_target_pairs={{0,12},{4,0},{8,4},{12,8},{1,13},{5,1},{9,5},{13,9},{2,14},{6,2},{... | collective-permute-start | bytes 1572872 | tf_op jit(solution)/shard_map/ppermute | solution.py:418
  64.5 1.8 collective-permute-start.1
  66.4 0.9 collective-permute-start.5
  67.3 3.0 %collective-permute-start.15 = (bf16[8,64,1024]{2,1,0:T(8,128)(2,1)S(1)}, bf16[8,64,1024]{2,1,0:T(8,128)(2,1)}, u32[]{:S(2)}, u32[]{:S(2)}) collective-permute-start(bf16[8,64,1024]{2,1,0:T(8,128)(2,1)S(1)} %copy-done.27), channel_id=1, source_target_pairs={{0,16},{16,0},{1,17},{17,1},{2,18},{18,2},{3,19},{19,3},{4,20},{20... | collective-permute-start | bytes 3145736 | tf_op jit(solution)/shard_map/ppermute | solution.py:418
  70.4 7.8 %collective-permute-done.11.refs_3_ = bf16[512,512]{1,0:T(8,128)(2,1)S(1)} collective-permute-done((bf16[512,512]{1,0:T(8,128)(2,1)}, bf16[512,512]{1,0:T(8,128)(2,1)S(1)}, u32[]{:S(2)}, u32[]{:S(2)}) %collective-permute-start.11) | collective-permute-done | bytes 524320 | tf_op jit(solution)/shard_map/ppermute | solution.py:418
  78.2 1.0 copy-done.6
  79.2 4.8 %lead_gram.1 = (f32[512,512]{1,0:T(8,128)}, bf16[8,512,512]{2,1,0:T(8,128)(2,1)S(1)}) custom-call(bf16[512,512]{1,0:T(8,128)(2,1)S(1)} %copy-done.6, bf16[512,512]{1,0:T(8,128)(2,1)S(1)} %copy-done.8, bf16[512,512]{1,0:T(8,128)(2,1)} %collective-permute-done.10.refs_2_, bf16[512,512]{1,0:T(8,128)(2,1)S(1)} %collective-permute-done.11.refs_3_, ...), custom_call_target="tpu_custom_call" | custom-call | flops 4294967296 | bytes 65536 | tf_op jit(solution)/shard_map/lead_gram/pallas_call | solution.py:117
  84.0 2.0 copy-done.9
  86.0 5.5 %collective-permute-start.17 = (f32[512,512]{1,0:T(8,128)}, f32[512,512]{1,0:T(8,128)}, u32[]{:S(2)}, u32[]{:S(2)}) collective-permute-start(f32[512,512]{1,0:T(8,128)} %get-tuple-element.42.g0), channel_id=1, source_target_pairs={{0,1},{1,0},{2,3},{3,2},{4,5},{5,4},{6,7},{7,6},{8,9},{9,8},{10,11... | collective-permute-start | bytes 3145736 | tf_op jit(solution)/shard_map/ppermute | solution.py:418
  92.3 8.3 %collective-permute-done.1.refs_2_ = bf16[1024,512]{1,0:T(8,128)(2,1)S(1)} collective-permute-done((bf16[1024,512]{1,0:T(8,128)(2,1)S(1)}, bf16[1024,512]{1,0:T(8,128)(2,1)S(1)}, u32[]{:S(2)}, u32[]{:S(2)}) %collective-permute-start.1) | collective-permute-done | bytes 1048608 | tf_op jit(solution)/shard_map/ppermute | solution.py:418
  101.2 1.0 copy-done.2
  102.1 2.7 %collective-permute-start.7 = (bf16[1024,512]{1,0:T(8,128)(2,1)}, bf16[1024,512]{1,0:T(8,128)(2,1)}, u32[]{:S(2)}, u32[]{:S(2)}) collective-permute-start(bf16[1024,512]{1,0:T(8,128)(2,1)} %copy-done.2), channel_id=1, source_target_pairs={{0,12},{4,0},{8,4},{12,8},{1,13},{5,1},{9,5},{13,9},{2,14},{6,2},{... | collective-permute-start | bytes 3145736 | tf_op jit(solution)/shard_map/ppermute | solution.py:418
  104.9 12.9 %chol_first.1 = (f32[512,512]{1,0:T(8,128)S(1)}, f32[512,512]{1,0:T(8,128)S(1)}) custom-call(f32[512,512]{1,0:T(8,128)} %get-tuple-element.42.g0, f32[512,512]{1,0:T(8,128)} %collective-permute-done.17.g1, f32[1,512]{1,0:T(1,128)S(1)} %bitcast.9), custom_call_target="tpu_custom_call" | custom-call | flops 85899345920 | bytes 65536 | tf_op jit(solution)/shard_map/chol_first/pallas_call | solution.py:196
  117.8 1.0 copy-done.22
  118.8 1.1 copy-done.24
  119.9 3.6 %collective-permute-done.6.refs_6_ = bf16[1024,512]{1,0:T(8,128)(2,1)} collective-permute-done((bf16[1024,512]{1,0:T(8,128)(2,1)S(1)}, bf16[1024,512]{1,0:T(8,128)(2,1)}, u32[]{:S(2)}, u32[]{:S(2)}) %collective-permute-start.6) | collective-permute-done | bytes 1048608 | tf_op jit(solution)/shard_map/ppermute | solution.py:418
  123.5 22.5 %collective-permute-done.2.refs_3_ = bf16[1024,512]{1,0:T(8,128)(2,1)} collective-permute-done((bf16[1024,512]{1,0:T(8,128)(2,1)S(1)}, bf16[1024,512]{1,0:T(8,128)(2,1)}, u32[]{:S(2)}, u32[]{:S(2)}) %collective-permute-start.2) | collective-permute-done | bytes 1048608 | tf_op jit(solution)/shard_map/ppermute | solution.py:418
  146.0 1.2 copy-done.3
  147.2 17.8 %gram_first.1 = (f32[1024,512]{1,0:T(8,128)S(1)}, f32[1024,512]{1,0:T(8,128)}, f32[1024,512]{1,0:T(8,128)}, f32[512,512]{1,0:T(8,128)S(1)}, f32[512,512]{1,0:T(8,128)S(1)}) custom-call(bf16[1024,512]{1,0:T(8,128)(2,1)S(1)} %bitcast.14, bf16[1024,512]{1,0:T(8,128)(2,1)} %collective-permute-done.refs_1_, bf16[1024,512]{1,0:T(8,128)(2,1)S(1)} %collective-permute-done.1.refs_2_, ...), custom_call_target="tpu_custom_call" | custom-call | flops 18253611008 | bytes 65536 | tf_op jit(solution)/shard_map/gram_first/pallas_call | solution.py:315
  165.1 4.2 %collective-permute-start.16 = (f32[1024,512]{1,0:T(8,128)}, f32[1024,512]{1,0:T(8,128)S(1)}, u32[]{:S(2)}, u32[]{:S(2)}) collective-permute-start(f32[1024,512]{1,0:T(8,128)} %get-tuple-element.41.rm), channel_id=1, source_target_pairs={{0,1},{1,0},{2,3},{3,2},{4,5},{5,4},{6,7},{7,6},{8,9},{9,8},{10,11... | collective-permute-start | bytes 6291464 | tf_op jit(solution)/shard_map/ppermute | solution.py:418
  169.3 10.6 %chol_second.1.inv_ref = f32[512,512]{1,0:T(8,128)S(1)} custom-call(f32[512,512]{1,0:T(8,128)S(1)} %copy-done.23, f32[512,512]{1,0:T(8,128)S(1)} %copy-done.25), custom_call_target="tpu_custom_call" | custom-call | flops 85899345920 | bytes 65536 | tf_op jit(solution)/shard_map/chol_second/pallas_call | solution.py:208
  180.0 5.0 %panel.1.refs_14_.p_ref = f32[1024,512]{1,0:T(8,128)S(1)} custom-call(f32[1024,512]{1,0:T(8,128)S(1)} %copy-done, f32[1024,512]{1,0:T(8,128)S(1)} %collective-permute-done.16.rr, f32[512,512]{1,0:T(8,128)S(1)} %chol_second.1.inv_ref, f32[1,512]{1,0:T(1,128)S(1)} %bitcast.10), custom_call_target="tpu_custom_call" | custom-call | flops 5368709120 | bytes 65536 | tf_op jit(solution)/shard_map/panel/pallas_call | solution.py:366
  185.0 1.4 copy-done.10
  186.4 1.0 copy-done.14
  187.4 1.2 copy-done.4
  188.6 1.2 copy-done.19
  189.9 1.2 copy-done.21
  191.1 14.7 %gram_second.1 = (f32[1024,512]{1,0:T(8,128)}, f32[1024,512]{1,0:T(8,128)}, f32[512,512]{1,0:T(8,128)S(1)}, f32[512,512]{1,0:T(8,128)}) custom-call(bf16[1024,512]{1,0:T(8,128)(2,1)S(1)} %bitcast.15, bf16[1024,512]{1,0:T(8,128)(2,1)} %collective-permute-done.refs_1_, bf16[1024,512]{1,0:T(8,128)(2,1)S(1)} %collective-permute-done.1.refs_2_, ...), custom_call_target="tpu_custom_call" | custom-call | flops 10737418240 | bytes 65536 | tf_op jit(solution)/shard_map/gram_second/pallas_call | solution.py:329
  205.8 1.0 copy-done.16
  207.3 5.1 %collective-permute-done.19.lr = f32[512,512]{1,0:T(8,128)} collective-permute-done((f32[512,512]{1,0:T(8,128)}, f32[512,512]{1,0:T(8,128)}, u32[]{:S(2)}, u32[]{:S(2)}) %collective-permute-start.19) | collective-permute-done | bytes 1048608 | tf_op jit(solution)/shard_map/ppermute | solution.py:418
  212.7 1.6 copy-done.11
  214.3 1.6 copy-done.12
  215.9 1.2 copy-done.15
  217.1 1.2 copy-done.17
  218.3 7.9 %final.1 = f32[1024,512]{1,0:T(8,128)S(1)} custom-call(f32[1024,512]{1,0:T(8,128)S(1)} %copy-done.12, f32[1024,512]{1,0:T(8,128)S(1)} %collective-permute-done.18.tr, f32[1024,512]{1,0:T(8,128)S(1)} %copy-done.11, f32[512,512]{1,0:T(8,128)S(1)} %copy-done.17, f32[512,512]{1,0:T(8,128)} %collective-permute-done.19.lr, f32[512,512]{1,0:T(8,128)S(1)} %copy-done.15, ...), custom_call_target="tpu_custom_call" | custom-call | flops 9663676416 | bytes 65536 | tf_op jit(solution)/shard_map/final/pallas_call | solution.py:403
  226.2 3.5 %copy.5 = f32[1,1024,1,512]{3,2,1,0:T(1,128)} copy(f32[1,1024,1,512]{3,1,2,0:T(8,128)S(1)} %bitcast.8) | data formatting | bytes 4194304 | tf_op jit(solution)/shard_map/reshape | solution.py:461
  (74 shorter events, 3.4 us)
Async XLA Ops:
  15.8 6.4 %copy-start.5 = (bf16[512,512]{1,0:T(8,128)(2,1)S(1)}, bf16[512,512]{1,0:T(8,128)(2,1)}, u32[]{:S(2)}) copy-start(bf16[512,512]{1,0:T(8,128)(2,1)} %get-tuple-element.30.refs_0_) | copy-start | bytes 1572868
  15.8 35.2 %copy-start.29 = (bf16[8,64,512]{2,1,0:T(8,128)(2,1)S(1)}, bf16[8,64,512]{2,1,0:T(8,128)(2,1)}, u32[]{:S(2)}) copy-start(bf16[8,64,512]{2,1,0:T(8,128)(2,1)} %get-tuple-element.28) | copy-start | bytes 1572868
  15.8 48.7 %copy-start.1 = (bf16[2,8,64,512]{3,2,1,0:T(8,128)(2,1)S(1)}, bf16[2,8,64,512]{3,2,1,0:T(8,128)(2,1)}, u32[]{:S(2)}) copy-start(bf16[2,8,64,512]{3,2,1,0:T(8,128)(2,1)} %get-tuple-element.27) | copy-start | bytes 3145732
  15.9 32.4 %all-to-all-start = ((bf16[8,64,1024]{2,1,0:T(8,128)(2,1)}), bf16[8,64,1024]{2,1,0:T(8,128)(2,1)S(1)}, u32[]{:S(2)}, u32[]{:S(2)}) async-start(bf16[8,64,1024]{2,1,0:T(8,128)(2,1)} %get-tuple-element.31), calls=%async_computation | async-start | bytes 2097152 | tf_op jit(solution)/shard_map/all_to_all | solution.py:434
  22.2 123.8 %all-gather.7.cloned.1.call-start = ((), (), s32[]{:S(2)}) async-start(), calls=%async_computation.2 | async-start | bytes 5242880 | tf_op jit(solution)/shard_map/all_gather | solution.py:443
  22.3 25.2 %collective-permute-start.10 = (bf16[512,512]{1,0:T(8,128)(2,1)S(1)}, bf16[512,512]{1,0:T(8,128)(2,1)}, u32[]{:S(2)}, u32[]{:S(2)}) collective-permute-start(bf16[512,512]{1,0:T(8,128)(2,1)S(1)} %copy-done.5), channel_id=1, source_target_pairs={{0,4},{4,8},{8,12},{12,0},{1,5},{5,9},{9,13},{13,1},{2,6},{6,10},{... | collective-permute-start | bytes 1572872 | tf_op jit(solution)/shard_map/ppermute | solution.py:418
  23.7 23.7 %collective-permute-start.8 = (bf16[512,512]{1,0:T(8,128)(2,1)S(1)}, bf16[512,512]{1,0:T(8,128)(2,1)}, u32[]{:S(2)}, u32[]{:S(2)}) collective-permute-start(bf16[512,512]{1,0:T(8,128)(2,1)S(1)} %copy-done.5), channel_id=1, source_target_pairs={{0,2},{2,0},{1,3},{3,1},{4,6},{6,4},{5,7},{7,5},{8,10},{10,8},{9,1... | collective-permute-start | bytes 1572872 | tf_op jit(solution)/shard_map/ppermute | solution.py:418
  24.9 22.5 %collective-permute-start.9 = (bf16[512,512]{1,0:T(8,128)(2,1)S(1)}, bf16[512,512]{1,0:T(8,128)(2,1)S(1)}, u32[]{:S(2)}, u32[]{:S(2)}) collective-permute-start(bf16[512,512]{1,0:T(8,128)(2,1)S(1)} %copy-done.5), channel_id=1, source_target_pairs={{0,12},{4,0},{8,4},{12,8},{1,13},{5,1},{9,5},{13,9},{2,14},{6,2},{... | collective-permute-start | bytes 1572872 | tf_op jit(solution)/shard_map/ppermute | solution.py:418
  49.3 138.1 %all-gather.5.cloned.1.call-start = ((), (), s32[]{:S(2)}) async-start(), calls=%async_computation.1 | async-start | bytes 5242880 | tf_op jit(solution)/shard_map/all_gather | solution.py:444
  49.3 18.0 %copy-start.27 = (bf16[8,64,1024]{2,1,0:T(8,128)(2,1)S(1)}, bf16[8,64,1024]{2,1,0:T(8,128)(2,1)}, u32[]{:S(2)}) copy-start(bf16[8,64,1024]{2,1,0:T(8,128)(2,1)} %copy-done.26) | copy-start | bytes 3145732
  49.3 28.8 %copy-start.8 = (bf16[512,512]{1,0:T(8,128)(2,1)S(1)}, bf16[512,512]{1,0:T(8,128)(2,1)}, u32[]{:S(2)}) copy-start(bf16[512,512]{1,0:T(8,128)(2,1)} %copy-done.7) | copy-start | bytes 1572868
  49.3 11.8 %collective-permute-start.12 = (bf16[512,512]{1,0:T(8,128)(2,1)}, bf16[512,512]{1,0:T(8,128)(2,1)S(1)}, u32[]{:S(2)}, u32[]{:S(2)}) collective-permute-start(bf16[512,512]{1,0:T(8,128)(2,1)} %collective-permute-done.8.refs_4_), channel_id=1, source_target_pairs={{0,12},{4,0},{8,4},{12,8},{1,13},{5,1},{9,5},{13,9},{2,14},{6,2},{... | collective-permute-start | bytes 1572872 | tf_op jit(solution)/shard_map/ppermute | solution.py:418
  51.0 13.5 %collective-permute-start.3 = (bf16[512,512]{1,0:T(8,128)(2,1)S(1)}, bf16[512,512]{1,0:T(8,128)(2,1)S(1)}, u32[]{:S(2)}, u32[]{:S(2)}) collective-permute-start(bf16[512,512]{1,0:T(8,128)(2,1)S(1)} %bitcast.18), channel_id=1, source_target_pairs={{0,2},{2,16},{16,18},{18,0},{1,3},{3,17},{17,19},{19,1},{4,6},{6,2... | collective-permute-start | bytes 1572872 | tf_op jit(solution)/shard_map/ppermute | solution.py:418
  52.0 14.4 %collective-permute-start.4 = (bf16[512,512]{1,0:T(8,128)(2,1)}, bf16[512,512]{1,0:T(8,128)(2,1)S(1)}, u32[]{:S(2)}, u32[]{:S(2)}) collective-permute-start(bf16[512,512]{1,0:T(8,128)(2,1)} %bitcast.2), channel_id=1, source_target_pairs={{0,18},{2,0},{16,2},{18,16},{1,19},{3,1},{17,3},{19,17},{4,22},{6,... | collective-permute-start | bytes 1572872 | tf_op jit(solution)/shard_map/ppermute | solution.py:418
  54.1 13.3 %collective-permute-start.13 = (bf16[512,512]{1,0:T(8,128)(2,1)}, bf16[512,512]{1,0:T(8,128)(2,1)S(1)}, u32[]{:S(2)}, u32[]{:S(2)}) collective-permute-start(bf16[512,512]{1,0:T(8,128)(2,1)} %collective-permute-done.8.refs_4_), channel_id=1, source_target_pairs={{0,4},{4,8},{8,12},{12,0},{1,5},{5,9},{9,13},{13,1},{2,6},{6,10},{... | collective-permute-start | bytes 1572872 | tf_op jit(solution)/shard_map/ppermute | solution.py:418
  55.2 23.0 %collective-permute-start.11 = (bf16[512,512]{1,0:T(8,128)(2,1)}, bf16[512,512]{1,0:T(8,128)(2,1)S(1)}, u32[]{:S(2)}, u32[]{:S(2)}) collective-permute-start(bf16[512,512]{1,0:T(8,128)(2,1)} %collective-permute-done.10.refs_2_), channel_id=1, source_target_pairs={{0,4},{4,8},{8,12},{12,0},{1,5},{5,9},{9,13},{13,1},{2,6},{6,10},{... | collective-permute-start | bytes 1572872 | tf_op jit(solution)/shard_map/ppermute | solution.py:418
  61.2 17.0 %collective-permute-start.14 = (bf16[512,512]{1,0:T(8,128)(2,1)S(1)}, bf16[512,512]{1,0:T(8,128)(2,1)S(1)}, u32[]{:S(2)}, u32[]{:S(2)}) collective-permute-start(bf16[512,512]{1,0:T(8,128)(2,1)S(1)} %collective-permute-done.12.refs_5_), channel_id=1, source_target_pairs={{0,12},{4,0},{8,4},{12,8},{1,13},{5,1},{9,5},{13,9},{2,14},{6,2},{... | collective-permute-start | bytes 1572872 | tf_op jit(solution)/shard_map/ppermute | solution.py:418
  64.5 36.0 %collective-permute-start.1 = (bf16[1024,512]{1,0:T(8,128)(2,1)S(1)}, bf16[1024,512]{1,0:T(8,128)(2,1)S(1)}, u32[]{:S(2)}, u32[]{:S(2)}) collective-permute-start(bf16[1024,512]{1,0:T(8,128)(2,1)S(1)} %bitcast.12), channel_id=1, source_target_pairs={{0,4},{4,8},{8,12},{12,0},{1,5},{5,9},{9,13},{13,1},{2,6},{6,10},{... | collective-permute-start | bytes 3145736 | tf_op jit(solution)/shard_map/ppermute | solution.py:418
  66.4 34.7 %collective-permute-start.5 = (bf16[1024,512]{1,0:T(8,128)(2,1)S(1)}, bf16[1024,512]{1,0:T(8,128)(2,1)S(1)}, u32[]{:S(2)}, u32[]{:S(2)}) collective-permute-start(bf16[1024,512]{1,0:T(8,128)(2,1)S(1)} %constant_dynamic-update-slice_fusion.refs_4_), channel_id=1, source_target_pairs={{0,12},{4,0},{8,4},{12,8},{1,13},{5,1},{9,5},{13,9},{2,14},{6,2},{... | collective-permute-start | bytes 3145736 | tf_op jit(solution)/shard_map/ppermute | solution.py:418
  67.3 34.8 %collective-permute-start.15 = (bf16[8,64,1024]{2,1,0:T(8,128)(2,1)S(1)}, bf16[8,64,1024]{2,1,0:T(8,128)(2,1)}, u32[]{:S(2)}, u32[]{:S(2)}) collective-permute-start(bf16[8,64,1024]{2,1,0:T(8,128)(2,1)S(1)} %copy-done.27), channel_id=1, source_target_pairs={{0,16},{16,0},{1,17},{17,1},{2,18},{18,2},{3,19},{19,3},{4,20},{20... | collective-permute-start | bytes 3145736 | tf_op jit(solution)/shard_map/ppermute | solution.py:418
  78.2 1.1 copy-start.6
  84.0 2.0 copy-start.9
  86.0 18.8 %collective-permute-start.17 = (f32[512,512]{1,0:T(8,128)}, f32[512,512]{1,0:T(8,128)}, u32[]{:S(2)}, u32[]{:S(2)}) collective-permute-start(f32[512,512]{1,0:T(8,128)} %get-tuple-element.42.g0), channel_id=1, source_target_pairs={{0,1},{1,0},{2,3},{3,2},{4,5},{5,4},{6,7},{7,6},{8,9},{9,8},{10,11... | collective-permute-start | bytes 3145736 | tf_op jit(solution)/shard_map/ppermute | solution.py:418
  91.6 28.3 %collective-permute-start = (bf16[1024,512]{1,0:T(8,128)(2,1)S(1)}, bf16[1024,512]{1,0:T(8,128)(2,1)}, u32[]{:S(2)}, u32[]{:S(2)}) collective-permute-start(bf16[1024,512]{1,0:T(8,128)(2,1)S(1)} %bitcast.13), channel_id=1, source_target_pairs={{0,12},{4,0},{8,4},{12,8},{1,13},{5,1},{9,5},{13,9},{2,14},{6,2},{... | collective-permute-start | bytes 3145736 | tf_op jit(solution)/shard_map/ppermute | solution.py:418
  100.5 23.0 %collective-permute-start.6 = (bf16[1024,512]{1,0:T(8,128)(2,1)S(1)}, bf16[1024,512]{1,0:T(8,128)(2,1)}, u32[]{:S(2)}, u32[]{:S(2)}) collective-permute-start(bf16[1024,512]{1,0:T(8,128)(2,1)S(1)} %constant_dynamic-update-slice_fusion.refs_4_), channel_id=1, source_target_pairs={{0,4},{4,8},{8,12},{12,0},{1,5},{5,9},{9,13},{13,1},{2,6},{6,10},{... | collective-permute-start | bytes 3145736 | tf_op jit(solution)/shard_map/ppermute | solution.py:418
  102.1 43.8 %collective-permute-start.2 = (bf16[1024,512]{1,0:T(8,128)(2,1)S(1)}, bf16[1024,512]{1,0:T(8,128)(2,1)}, u32[]{:S(2)}, u32[]{:S(2)}) collective-permute-start(bf16[1024,512]{1,0:T(8,128)(2,1)S(1)} %collective-permute-done.1.refs_2_), channel_id=1, source_target_pairs={{0,4},{4,8},{8,12},{12,0},{1,5},{5,9},{9,13},{13,1},{2,6},{6,10},{... | collective-permute-start | bytes 3145736 | tf_op jit(solution)/shard_map/ppermute | solution.py:418
  102.1 43.8 %collective-permute-start.7 = (bf16[1024,512]{1,0:T(8,128)(2,1)}, bf16[1024,512]{1,0:T(8,128)(2,1)}, u32[]{:S(2)}, u32[]{:S(2)}) collective-permute-start(bf16[1024,512]{1,0:T(8,128)(2,1)} %copy-done.2), channel_id=1, source_target_pairs={{0,12},{4,0},{8,4},{12,8},{1,13},{5,1},{9,5},{13,9},{2,14},{6,2},{... | collective-permute-start | bytes 3145736 | tf_op jit(solution)/shard_map/ppermute | solution.py:418
  117.8 1.0 copy-start.22
  118.8 1.1 copy-start.24
  146.0 1.2 copy-start.3
  147.2 22.1 %copy-start.23 = (f32[512,512]{1,0:T(8,128)S(1)}, f32[512,512]{1,0:T(8,128)}, u32[]{:S(2)}) copy-start(f32[512,512]{1,0:T(8,128)} %copy-done.22) | copy-start | bytes 3145732
  147.2 22.1 %copy-start.25 = (f32[512,512]{1,0:T(8,128)S(1)}, f32[512,512]{1,0:T(8,128)}, u32[]{:S(2)}) copy-start(f32[512,512]{1,0:T(8,128)} %copy-done.24) | copy-start | bytes 3145732
  165.0 14.9 %copy-start.13 = (f32[1024,512]{1,0:T(8,128)}, f32[1024,512]{1,0:T(8,128)S(1)}, u32[]{:S(2)}) copy-start(f32[1024,512]{1,0:T(8,128)S(1)} %get-tuple-element.37.refs_10_) | copy-start | bytes 6291460
  165.0 14.9 %copy-start.18 = (f32[512,512]{1,0:T(8,128)}, f32[512,512]{1,0:T(8,128)S(1)}, u32[]{:S(2)}) copy-start(f32[512,512]{1,0:T(8,128)S(1)} %get-tuple-element.39.refs_12_) | copy-start | bytes 3145732
  165.1 14.9 %copy-start.20 = (f32[512,512]{1,0:T(8,128)}, f32[512,512]{1,0:T(8,128)S(1)}, u32[]{:S(2)}) copy-start(f32[512,512]{1,0:T(8,128)S(1)} %get-tuple-element.40.refs_13_) | copy-start | bytes 3145732
  165.1 14.9 %collective-permute-start.16 = (f32[1024,512]{1,0:T(8,128)}, f32[1024,512]{1,0:T(8,128)S(1)}, u32[]{:S(2)}, u32[]{:S(2)}) collective-permute-start(f32[1024,512]{1,0:T(8,128)} %get-tuple-element.41.rm), channel_id=1, source_target_pairs={{0,1},{1,0},{2,3},{3,2},{4,5},{5,4},{6,7},{7,6},{8,9},{9,8},{10,11... | collective-permute-start | bytes 6291464 | tf_op jit(solution)/shard_map/ppermute | solution.py:418
  169.3 10.6 %copy-start = (f32[1024,512]{1,0:T(8,128)S(1)}, f32[1024,512]{1,0:T(8,128)}, u32[]{:S(2)}) copy-start(f32[1024,512]{1,0:T(8,128)} %get-tuple-element.41.rm) | copy-start | bytes 6291460
  185.0 1.4 copy-start.10
  187.4 1.2 copy-start.4
  188.6 1.2 copy-start.19
  189.9 1.2 copy-start.21
  191.1 16.2 %copy-start.28 = (f32[8192]{0:T(1024)S(1)}, f32[8192]{0:T(1024)}, u32[]{:S(2)}) copy-start(f32[8192]{0:T(1024)} %param.3) | copy-start | bytes 98308
  206.8 5.9 %collective-permute-start.18 = (f32[1024,512]{1,0:T(8,128)}, f32[1024,512]{1,0:T(8,128)S(1)}, u32[]{:S(2)}, u32[]{:S(2)}) collective-permute-start(f32[1024,512]{1,0:T(8,128)} %get-tuple-element.46), channel_id=1, source_target_pairs={{0,1},{1,0},{2,3},{3,2},{4,5},{5,4},{6,7},{7,6},{8,9},{9,8},{10,11... | collective-permute-start | bytes 6291464 | tf_op jit(solution)/shard_map/ppermute | solution.py:418
  206.8 5.6 %collective-permute-start.19 = (f32[512,512]{1,0:T(8,128)}, f32[512,512]{1,0:T(8,128)}, u32[]{:S(2)}, u32[]{:S(2)}) collective-permute-start(f32[512,512]{1,0:T(8,128)} %get-tuple-element.48), channel_id=1, source_target_pairs={{0,1},{1,0},{2,3},{3,2},{4,5},{5,4},{6,7},{7,6},{8,9},{9,8},{10,11... | collective-permute-start | bytes 3145736 | tf_op jit(solution)/shard_map/ppermute | solution.py:418
  212.7 1.6 copy-start.11
  214.3 1.6 copy-start.12
  215.9 1.2 copy-start.15
  217.1 1.2 copy-start.17
  (5 other events, 4.8 us)
Sparse Core Ops, SparseCore 0:
  49.4 50.4 all-gather.6
  105.0 50.3 all-gather.4

commit v2 on v1

--- a/solution.py
+++ b/solution.py
@@ -218,7 +218,8 @@
 
 
 TALL = jax.ShapeDtypeStruct((1024, 512), F32)
-ORDER = tuple((dx, dz) for dz in range(2) for dx in (0, 1, 3, 2))
+NEAR = tuple((dx, dz) for dz in range(2) for dx in (0, 1, 3))
+FAR = ((2, 0), (2, 1))
 
 
 def fetch(b_ref, b_s, sems):
@@ -245,17 +246,25 @@
     return rows, total
 
 
-def row_products(a_in, b_s, lanes):
+def row_products(a_in, order, b_s, lanes):
     total = None
-    for ref, (dx, dz) in zip(a_in, ORDER):
+    for ref, (dx, dz) in zip(a_in, order):
         term = nn(ref[:, lanes], b_s[place(dx, dz)].reshape(256, 1024))
         total = term if total is None else total + term
     return total
 
 
+def side_products(a_in, order, l_ref):
+    total = None
+    for ref, (dx, dz) in zip(a_in, order):
+        term = nt(ref[...], l_ref[place(dx, dz)])
+        total = term if total is None else total + term
+    return total
+
+
 def first_kernel(*refs):
-    a_in, l_ref, b_ref = refs[:8], refs[8], refs[9]
-    own, other, rl, lc_own, lc_other, b_s, sems = refs[10:]
+    a_in, l_ref, b_ref = refs[:6], refs[6], refs[7]
+    own, other, rl, lc_own, lc_other, far_ref, b_s, sems = refs[9:]
     lanes = half_lanes(0)
 
     @pl.when(pl.program_id(0) == 0)
@@ -269,21 +278,27 @@
             return 0
 
         lax.fori_loop(0, 2, step, 0)
-
-    tile = row_products(a_in, b_s, lanes)
+        for dz in range(2):
+            far_ref[dz] = b_s[place(2, dz)].reshape(256, 1024)
+
+    tile = row_products(a_in, NEAR, b_s, lanes)
     own[...] = tile[:, :512]
     other[...] = tile[:, 512:]
-    side = None
-    for ref, (dx, dz) in zip(a_in, ORDER):
-        term = nt(ref[...], l_ref[place(dx, dz)])
-        side = term if side is None else side + term
-    rl[...] = side
+    rl[...] = side_products(a_in, NEAR, l_ref)
+
+
+def middle_kernel(a0, a1, l_ref, far_ref, own0, other0, rl0, own, other, rl):
+    lanes = half_lanes(0)
+    tile = nn(a0[:, lanes], far_ref[0]) + nn(a1[:, lanes], far_ref[1])
+    own[...] = own0[...] + tile[:, :512]
+    other[...] = other0[...] + tile[:, 512:]
+    rl[...] = rl0[...] + side_products((a0, a1), FAR, l_ref)
 
 
 def second_kernel(*refs):
     a_in, l_ref, b_ref = refs[:8], refs[8], refs[9]
     own0, other0, lc_own0, lc_other0 = refs[10:14]
-    own, other, lc_own, lc_other, b_s, sems = refs[15:]
+    own, other, lc_own, lc_other, b_s, sems = refs[14:]
     lanes = half_lanes(1)
 
     @pl.when(pl.program_id(0) == 0)
@@ -298,7 +313,7 @@
 
         lax.fori_loop(0, 2, step, 0)
 
-    tile = row_products(a_in, b_s, lanes)
+    tile = row_products(a_in, NEAR + FAR, b_s, lanes)
     own[...] = own0[...] + tile[:, :512]
     other[...] = other0[...] + tile[:, 512:]
 
@@ -311,36 +326,48 @@
 SCRATCH = [pltpu.VMEM((8, 4, 64, 1024), BF), pltpu.SemaphoreType.DMA((4,))]
 
 
-def gram_first(a, lead, b):
+def gram_first(a, lead, b, after):
     return pl.pallas_call(
         first_kernel,
         grid=(4,),
-        in_specs=[BLOCK] * 8 + [once(8, 512, 512), ANY],
-        out_specs=[BLOCK] * 3 + [once(512, 512)] * 2,
-        out_shape=[TALL] * 3 + [SQUARE] * 2,
+        in_specs=[BLOCK] * 6 + [once(8, 512, 512), ANY, ANY],
+        out_specs=[BLOCK] * 3 + [once(512, 512)] * 2 + [once(2, 256, 1024)],
+        out_shape=[TALL] * 3 + [SQUARE] * 2 + [jax.ShapeDtypeStruct((2, 256, 1024), BF)],
         scratch_shapes=SCRATCH,
         compiler_params=params(40),
         cost_estimate=cost(17),
         name="gram_first",
-    )(*a, lead, b)
-
-
-def gram_second(a, lead, b, own, other, lc_own, lc_other, after):
+    )(*a, lead, b, after)
+
+
+def gram_middle(a, lead, far, own, other, rl):
+    return pl.pallas_call(
+        middle_kernel,
+        grid=(4,),
+        in_specs=[BLOCK] * 2 + [once(8, 512, 512), once(2, 256, 1024)] + [BLOCK] * 3,
+        out_specs=[BLOCK] * 3,
+        out_shape=[TALL] * 3,
+        compiler_params=params(40),
+        cost_estimate=cost(5),
+        name="gram_middle",
+    )(*a, lead, far, own, other, rl)
+
+
+def gram_second(a, lead, b, own, other, lc_own, lc_other):
     return pl.pallas_call(
         second_kernel,
         grid=(4,),
         in_specs=[BLOCK] * 8
         + [once(8, 512, 512), ANY]
         + [BLOCK] * 2
-        + [once(512, 512)] * 2
-        + [ANY],
+        + [once(512, 512)] * 2,
         out_specs=[BLOCK] * 2 + [once(512, 512)] * 2,
         out_shape=[TALL] * 2 + [SQUARE] * 2,
         scratch_shapes=SCRATCH,
         compiler_params=params(40),
         cost_estimate=cost(10),
         name="gram_second",
-    )(*a, lead, b, own, other, lc_own, lc_other, after)
+    )(*a, lead, b, own, other, lc_own, lc_other)
 
 
 def column_of(lane):
@@ -392,11 +419,11 @@
     c = (tm[...] + tr[...]) * scale + jnp.where(
         row_of(pl.program_id(0)) == col, sc_ref[...], 0.0
     )
-    out_ref[...] = c - nn(p, u_ref[...], HI)
+    out_ref[:, 0, :] = c - nn(p, u_ref[...], HI)
 
     @pl.when(k == 0)
     def _():
-        out_ref[:, :256] = jnp.where(core == 0, p[:, :256], p[:, 256:])
+        out_ref[:, 0, :256] = jnp.where(core == 0, p[:, :256], p[:, 256:])
 
 
 def final(tm, tr, p, lm, lr, inv, sc):
@@ -404,8 +431,8 @@
         final_kernel,
         grid=(4,),
         in_specs=[BLOCK] * 3 + [once(512, 512)] * 3 + [once(1, 512)],
-        out_specs=BLOCK,
-        out_shape=TALL,
+        out_specs=pl.BlockSpec((256, 1, 512), lambda m: (m, 0, 0)),
+        out_shape=jax.ShapeDtypeStruct((1024, 1, 512), F32),
         scratch_shapes=[pltpu.VMEM((512, 512), F32)],
         compiler_params=params(32),
         cost_estimate=cost(9),
@@ -442,6 +469,7 @@
     cols_z = shift(cols, "zh", 1)
     b_own = lax.all_gather(cols, "y")
     b_z = lax.all_gather(cols_z, "y")
+    rows = after(rows, lead_z)
     a_up, a_down = near(rows, "x")
     az_up, az_down = near(rows_z, "x")
     g, lead_all = lead_gram([lead, l_up, l_down, l_far, lead_z, lz_up, lz_down, lz_far])
@@ -450,11 +478,12 @@
     inv = chol_rest(half_a, half_inv)
     a_far, az_far = shift(a_down, "x", 1), shift(az_up, "x", -1)
 
-    a = [rows, a_up, a_down, a_far, rows_z, az_up, az_down, az_far]
-    parts = gram_first(a, lead_all, b_own)
-    rl = parts[2]
+    a = [rows, a_up, a_down, rows_z, az_up, az_down]
+    own, other, rl, lc_own, lc_other, b_part = gram_first(a, lead_all, b_own, inv)
+    own, other, rl = gram_middle([a_far, az_far], lead_all, b_part, own, other, rl)
     p = panel(rl, shift(rl, "core", 1), inv, sl)
-    own, other, lc_own, lc_other = gram_second(a, lead_all, b_z, *parts[:2], *parts[3:], p)
+    a = [*a, a_far, az_far]
+    own, other, lc_own, lc_other = gram_second(a, lead_all, b_z, own, other, lc_own, lc_other)
     sc = lax.dynamic_slice(shrink.reshape(2, 16, 256), (0, 2 * k + core, 0), (2, 1, 256))
     sc = sc.reshape(1, 512)
     out = final(own, shift(other, "core", 1), p, lc_own, shift(lc_other, "core", 1), inv, sc)

time: 237 us -> 202 us (0.85)
  waiting for transfers between devices: 74.7 us -> 46.4 us
  local copies, waits for them, and re-layouts: 26.1 us -> 15.4 us
  Pallas kernels: 83.1 us -> 88.1 us
    ppermute x20, waiting for transfers between devices: 74.7 us -> 46.3 us  [shift(): return lax.ppermute(v, axis, [(i, (i + by) % n) for i in range(n)])]
    unnamed x61 -> x37, local copies, waits for them, and re-layouts: 21.9 us -> 13.9 us
    pallas_call x1 -> x2, Pallas kernels: 17.8 us -> 22.5 us  [the longest x1 16.3 us: gram_first(): pl.pallas_call(first_kernel, grid=(4,), in_specs=[BLOCK] * 6 + [once(8, 5...]
    reshape x1 -> x0, local copies, waits for them, and re-layouts: 3.48 us -> none  [body(): return out.reshape(1, 1024, 1, 512)]
  transfers between devices with their start and end apart: 23 -> 23, of which waited for: 9 -> 9; matrix products, arithmetic and copies ran while one was open for 0% -> 1% of each run, Pallas kernels for 22% -> 34%
where the time goes in v2:
time: 202 us; the launch traced here: 201 us
  Pallas kernels  88.1 us (44%)
  waiting for transfers between devices  46.4 us (23%)
  starting transfers between devices  37.5 us (19%)
  local copies, waits for them, and re-layouts  15.4 us (8%)
  between operations  13.7 us (7%)
    ppermute x20, waiting for transfers between devices, shift(): return lax.ppermute(v, axis, [(i, (i + by) % n) for i in range(n)])  46.3 us
    ppermute x20, starting transfers between devices, shift(): return lax.ppermute(v, axis, [(i, (i + by) % n) for i in range(n)])  31.1 us
    pallas_call x1, Pallas kernels, gram_first(): pl.pallas_call(first_kernel, grid=(4,), in_specs=[BLOCK] * 6 + [once(8, 5...  16.3 us
    pallas_call x1, Pallas kernels, gram_second(): pl.pallas_call(second_kernel, grid=(4,), in_specs=[BLOCK] * 8 + [once(8,...  15.6 us
    unnamed x37, local copies, waits for them, and re-layouts  13.9 us
    pallas_call x1, Pallas kernels, chol_half(): pl.pallas_call(chol_first, in_specs=[VM] * 3, out_specs=[VM, VM], out_sha...  11.3 us
    pallas_call x1, Pallas kernels, chol_rest(): pl.pallas_call(chol_second, in_specs=[VM, VM], out_specs=VM, out_shape=SQ...  10.8 us
    pallas_call x1, Pallas kernels, final(): pl.pallas_call(final_kernel, grid=(4,), in_specs=[BLOCK] * 3 + [once(512,...  9.54 us
  transfers between devices with their start and end apart: 23, of which 9 were waited for; matrix products, arithmetic and copies ran while one was open for 1% of the time, Pallas kernels for 34%

profile of v2, /device:TPU:1, one launch (start us, length us, event | category | flops | bytes accessed | tf_op | source)
XLA Modules:
  0.0 201.1 jit_solution(14791277997787604285)
XLA Ops:
  6.5 9.3 %prep.1 = (bf16[2,8,64,512]{3,2,1,0:T(8,128)(2,1)}, bf16[8,64,512]{2,1,0:T(8,128)(2,1)}, bf16[8,64,512]{2,1,0:T(8,128)(2,1)}, bf16[512,512]{1,0:T(8,128)(2,1)}, bf16[8,64,1024]{2,1,0:T(8,128)(2,1)}) custom-call(bf16[512,8192]{1,0:T(8,128)(2,1)} %hi_ref.1, bf16[512,8192]{1,0:T(8,128)(2,1)} %hi_ref.1), custom_call_target="tpu_custom_call" | custom-call | flops 9663676416 | bytes 65536 | tf_op jit(solution)/shard_map/prep/pallas_call | solution.py:70
  15.9 6.3 %all-to-all-start = ((bf16[8,64,1024]{2,1,0:T(8,128)(2,1)}), bf16[8,64,1024]{2,1,0:T(8,128)(2,1)}, u32[]{:S(2)}, u32[]{:S(2)}) async-start(bf16[8,64,1024]{2,1,0:T(8,128)(2,1)} %get-tuple-element.34), calls=%async_computation | async-start | bytes 2097152 | tf_op jit(solution)/shard_map/all_to_all | solution.py:461
  22.3 1.5 collective-permute-start
  23.8 2.4 %collective-permute-start.1 = (bf16[512,512]{1,0:T(8,128)(2,1)S(1)}, bf16[512,512]{1,0:T(8,128)(2,1)S(1)}, u32[]{:S(2)}, u32[]{:S(2)}) collective-permute-start(bf16[512,512]{1,0:T(8,128)(2,1)S(1)} %copy-done), channel_id=1, source_target_pairs={{0,12},{4,0},{8,4},{12,8},{1,13},{5,1},{9,5},{13,9},{2,14},{6,2},{... | collective-permute-start | bytes 1572872 | tf_op jit(solution)/shard_map/ppermute | solution.py:445
  26.2 20.0 %collective-permute-done.refs_4_ = bf16[512,512]{1,0:T(8,128)(2,1)S(1)} collective-permute-done((bf16[512,512]{1,0:T(8,128)(2,1)S(1)}, bf16[512,512]{1,0:T(8,128)(2,1)S(1)}, u32[]{:S(2)}, u32[]{:S(2)}) %collective-permute-start) | collective-permute-done | bytes 524320 | tf_op jit(solution)/shard_map/ppermute | solution.py:445
  46.1 0.1 collective-permute-done.1.refs_1_
  46.3 1.1 collective-permute-done.2.refs_2_
  47.4 0.0 all-gather.5.cloned.1.call-start
  47.4 1.7 collective-permute-start.12
  49.1 0.9 collective-permute-start.5
  50.1 2.2 %collective-permute-start.6 = (bf16[512,512]{1,0:T(8,128)(2,1)S(1)}, bf16[512,512]{1,0:T(8,128)(2,1)S(1)}, u32[]{:S(2)}, u32[]{:S(2)}) collective-permute-start(bf16[512,512]{1,0:T(8,128)(2,1)S(1)} %bitcast.13), channel_id=1, source_target_pairs={{0,18},{2,0},{16,2},{18,16},{1,19},{3,1},{17,3},{19,17},{4,22},{6,... | collective-permute-start | bytes 1572872 | tf_op jit(solution)/shard_map/ppermute | solution.py:445
  52.2 1.1 collective-permute-start.13
  53.4 5.6 %collective-permute-done.12.refs_5_ = bf16[512,512]{1,0:T(8,128)(2,1)S(1)} collective-permute-done((bf16[512,512]{1,0:T(8,128)(2,1)S(1)}, bf16[512,512]{1,0:T(8,128)(2,1)S(1)}, u32[]{:S(2)}, u32[]{:S(2)}) %collective-permute-start.12) | collective-permute-done | bytes 524320 | tf_op jit(solution)/shard_map/ppermute | solution.py:445
  59.0 3.1 %collective-permute-start.14 = (bf16[512,512]{1,0:T(8,128)(2,1)S(1)}, bf16[512,512]{1,0:T(8,128)(2,1)S(1)}, u32[]{:S(2)}, u32[]{:S(2)}) collective-permute-start(bf16[512,512]{1,0:T(8,128)(2,1)S(1)} %collective-permute-done.12.refs_5_), channel_id=1, source_target_pairs={{0,12},{4,0},{8,4},{12,8},{1,13},{5,1},{9,5},{13,9},{2,14},{6,2},{... | collective-permute-start | bytes 1572872 | tf_op jit(solution)/shard_map/ppermute | solution.py:445
  62.1 0.5 collective-permute-done.5
  62.6 0.8 constant_dynamic-update-slice_fusion.1
  63.5 0.8 constant_dynamic-update-slice_fusion.refs_3_
  64.3 1.4 collective-permute-start.7
  65.6 2.4 %collective-permute-start.15 = (bf16[8,64,1024]{2,1,0:T(8,128)(2,1)}, bf16[8,64,1024]{2,1,0:T(8,128)(2,1)}, u32[]{:S(2)}, u32[]{:S(2)}) collective-permute-start(bf16[8,64,1024]{2,1,0:T(8,128)(2,1)} %all-to-all-done), channel_id=1, source_target_pairs={{0,16},{16,0},{1,17},{17,1},{2,18},{18,2},{3,19},{19,3},{4,20},{20... | collective-permute-start | bytes 3145736 | tf_op jit(solution)/shard_map/ppermute | solution.py:445
  68.0 0.5 collective-permute-start.4
  68.6 7.6 %collective-permute-done.11.refs_3_ = bf16[512,512]{1,0:T(8,128)(2,1)S(1)} collective-permute-done((bf16[512,512]{1,0:T(8,128)(2,1)S(1)}, bf16[512,512]{1,0:T(8,128)(2,1)S(1)}, u32[]{:S(2)}, u32[]{:S(2)}) %collective-permute-start.11) | collective-permute-done | bytes 524320 | tf_op jit(solution)/shard_map/ppermute | solution.py:445
  76.2 2.6 %lead_gram.1 = (f32[512,512]{1,0:T(8,128)S(1)}, bf16[8,512,512]{2,1,0:T(8,128)(2,1)S(1)}) custom-call(bf16[512,512]{1,0:T(8,128)(2,1)S(1)} %copy-done, bf16[512,512]{1,0:T(8,128)(2,1)S(1)} %collective-permute-done.1.refs_1_, bf16[512,512]{1,0:T(8,128)(2,1)S(1)} %collective-permute-done.2.refs_2_, bf16[512,512]{1,0:T(8,128)(2,1)S(1)} %collective-permute-done.11.refs_3_, ...), custom_call_target="tpu_custom_call" | custom-call | flops 4294967296 | bytes 65536 | tf_op jit(solution)/shard_map/lead_gram/pallas_call | solution.py:117
  78.9 2.0 copy-done.1
  80.9 5.4 %collective-permute-start.16 = (f32[512,512]{1,0:T(8,128)S(1)}, f32[512,512]{1,0:T(8,128)S(1)}, u32[]{:S(2)}, u32[]{:S(2)}) collective-permute-start(f32[512,512]{1,0:T(8,128)S(1)} %get-tuple-element.43.g0), channel_id=1, source_target_pairs={{0,1},{1,0},{2,3},{3,2},{4,5},{5,4},{6,7},{7,6},{8,9},{9,8},{10,11... | collective-permute-start | bytes 3145736 | tf_op jit(solution)/shard_map/ppermute | solution.py:445
  86.2 0.7 slice.3
  86.9 6.4 %collective-permute-done.7.refs_4_ = bf16[1024,512]{1,0:T(8,128)(2,1)} collective-permute-done((bf16[1024,512]{1,0:T(8,128)(2,1)}, bf16[1024,512]{1,0:T(8,128)(2,1)}, u32[]{:S(2)}, u32[]{:S(2)}) %collective-permute-start.7) | collective-permute-done | bytes 1048608 | tf_op jit(solution)/shard_map/ppermute | solution.py:445
  93.4 3.4 %collective-permute-start.3 = (bf16[1024,512]{1,0:T(8,128)(2,1)}, bf16[1024,512]{1,0:T(8,128)(2,1)}, u32[]{:S(2)}, u32[]{:S(2)}) collective-permute-start(bf16[1024,512]{1,0:T(8,128)(2,1)} %bitcast.refs_0_), channel_id=1, source_target_pairs={{0,12},{4,0},{8,4},{12,8},{1,13},{5,1},{9,5},{13,9},{2,14},{6,2},{... | collective-permute-start | bytes 3145736 | tf_op jit(solution)/shard_map/ppermute | solution.py:445
  96.8 1.9 collective-permute-done.4.refs_2_
  98.7 1.5 collective-permute-start.9
  100.2 11.3 %chol_first.1 = (f32[512,512]{1,0:T(8,128)S(1)}, f32[512,512]{1,0:T(8,128)S(1)}) custom-call(f32[512,512]{1,0:T(8,128)S(1)} %get-tuple-element.43.g0, f32[512,512]{1,0:T(8,128)S(1)} %collective-permute-done.16.g1, f32[1,512]{1,0:T(1,128)S(1)} %bitcast.8), custom_call_target="tpu_custom_call" | custom-call | flops 85899345920 | bytes 65536 | tf_op jit(solution)/shard_map/chol_first/pallas_call | solution.py:196
  111.5 10.8 %chol_second.1.refs_8_.inv_ref = f32[512,512]{1,0:T(8,128)S(1)} custom-call(f32[512,512]{1,0:T(8,128)S(1)} %get-tuple-element.44.a0, f32[512,512]{1,0:T(8,128)S(1)} %get-tuple-element.45.i0), custom_call_target="tpu_custom_call" | custom-call | flops 85899345920 | bytes 65536 | tf_op jit(solution)/shard_map/chol_second/pallas_call | solution.py:208
  122.4 16.3 %gram_first.1 = (f32[1024,512]{1,0:T(8,128)S(1)}, f32[1024,512]{1,0:T(8,128)}, f32[1024,512]{1,0:T(8,128)}, f32[512,512]{1,0:T(8,128)S(1)}, f32[512,512]{1,0:T(8,128)S(1)}, /*index=5*/bf16[2,256,1024]{2,1,0:T(8,128)(2,1)S(1)}) custom-call(bf16[1024,512]{1,0:T(8,128)(2,1)} %bitcast.refs_0_, bf16[1024,512]{1,0:T(8,128)(2,1)} %collective-permute-done.3.refs_1_, ...), custom_call_target="tpu_custom_call" | custom-call | flops 18253611008 | bytes 65536 | tf_op jit(solution)/shard_map/gram_first/pallas_call | solution.py:330
  138.7 1.0 copy-done.11
  139.7 1.0 copy-done.13
  140.7 3.0 %collective-permute-done.9.a0.refs_6_ = bf16[1024,512]{1,0:T(8,128)(2,1)} collective-permute-done((bf16[1024,512]{1,0:T(8,128)(2,1)}, bf16[1024,512]{1,0:T(8,128)(2,1)}, u32[]{:S(2)}, u32[]{:S(2)}) %collective-permute-start.9) | collective-permute-done | bytes 1048608 | tf_op jit(solution)/shard_map/ppermute | solution.py:445
  143.6 1.6 copy-done.4
  145.2 6.2 %gram_middle.1 = (f32[1024,512]{1,0:T(8,128)S(1)}, f32[1024,512]{1,0:T(8,128)S(1)}, f32[1024,512]{1,0:T(8,128)S(1)}) custom-call(bf16[1024,512]{1,0:T(8,128)(2,1)} %collective-permute-done.9.a0.refs_6_, bf16[1024,512]{1,0:T(8,128)(2,1)} %collective-permute-done.10.a1.refs_7_, bf16[8,512,512]{2,1,0:T(8,128)(2,1)} %copy-done.1, ...), custom_call_target="tpu_custom_call" | custom-call | flops 5368709120 | bytes 65536 | tf_op jit(solution)/shard_map/gram_middle/pallas_call | solution.py:344
  151.4 1.3 copy-done.2
  152.7 1.4 copy-done.3
  154.1 3.1 %collective-permute-start.18 = (f32[1024,512]{1,0:T(8,128)S(1)}, f32[1024,512]{1,0:T(8,128)}, u32[]{:S(2)}, u32[]{:S(2)}) collective-permute-start(f32[1024,512]{1,0:T(8,128)S(1)} %get-tuple-element.56.rm), channel_id=1, source_target_pairs={{0,1},{1,0},{2,3},{3,2},{4,5},{5,4},{6,7},{7,6},{8,9},{9,8},{10,11... | collective-permute-start | bytes 6291464 | tf_op jit(solution)/shard_map/ppermute | solution.py:445
  157.3 1.2 copy-done.12
  158.5 1.2 copy-done.14
  159.7 15.6 %gram_second.1 = (f32[1024,512]{1,0:T(8,128)}, f32[1024,512]{1,0:T(8,128)}, f32[512,512]{1,0:T(8,128)S(1)}, f32[512,512]{1,0:T(8,128)S(1)}) custom-call(bf16[1024,512]{1,0:T(8,128)(2,1)} %bitcast.refs_0_, bf16[1024,512]{1,0:T(8,128)(2,1)} %collective-permute-done.3.refs_1_, bf16[1024,512]{1,0:T(8,128)(2,1)} %collective-permute-done.4.refs_2_, ...), custom_call_target="tpu_custom_call" | custom-call | flops 10737418240 | bytes 65536 | tf_op jit(solution)/shard_map/gram_second/pallas_call | solution.py:357
  175.3 1.0 copy-done.9
  176.3 0.5 collective-permute-start.19
  176.9 1.4 copy-done.7
  178.2 6.4 %panel.1.p_ref = f32[1024,512]{1,0:T(8,128)S(1)} custom-call(f32[1024,512]{1,0:T(8,128)S(1)} %get-tuple-element.56.rm, f32[1024,512]{1,0:T(8,128)} %collective-permute-done.18.rr, f32[512,512]{1,0:T(8,128)S(1)} %copy-done.7, f32[1,512]{1,0:T(1,128)S(1)} %bitcast.9), custom_call_target="tpu_custom_call" | custom-call | flops 5368709120 | bytes 65536 | tf_op jit(solution)/shard_map/panel/pallas_call | solution.py:393
  184.7 9.5 %final.1 = f32[1024,1,512]{2,1,0:T(1,128)} custom-call(f32[1024,512]{1,0:T(8,128)S(1)} %copy-done.5, f32[1024,512]{1,0:T(8,128)} %collective-permute-done.17.tr, f32[1024,512]{1,0:T(8,128)S(1)} %panel.1.p_ref, f32[512,512]{1,0:T(8,128)S(1)} %copy-done.10, f32[512,512]{1,0:T(8,128)} %collective-permute-done.19.lr, f32[512,512]{1,0:T(8,128)S(1)} %copy-done.8, ...), custom_call_target="tpu_custom_call" | custom-call | flops 9663676416 | bytes 65536 | tf_op jit(solution)/shard_map/final/pallas_call | solution.py:430
  (50 shorter events, 0.2 us)
Async XLA Ops:
  15.8 6.4 %copy-start = (bf16[512,512]{1,0:T(8,128)(2,1)S(1)}, bf16[512,512]{1,0:T(8,128)(2,1)}, u32[]{:S(2)}) copy-start(bf16[512,512]{1,0:T(8,128)(2,1)} %get-tuple-element.33.refs_0_) | copy-start | bytes 1572868
  15.8 33.3 %copy-start.17 = (bf16[8,64,512]{2,1,0:T(8,128)(2,1)S(1)}, bf16[8,64,512]{2,1,0:T(8,128)(2,1)}, u32[]{:S(2)}) copy-start(bf16[8,64,512]{2,1,0:T(8,128)(2,1)} %get-tuple-element.37) | copy-start | bytes 1572868
  15.9 34.2 %copy-start.16 = (bf16[8,64,512]{2,1,0:T(8,128)(2,1)S(1)}, bf16[8,64,512]{2,1,0:T(8,128)(2,1)}, u32[]{:S(2)}) copy-start(bf16[8,64,512]{2,1,0:T(8,128)(2,1)} %get-tuple-element.38) | copy-start | bytes 1572868
  15.9 31.5 %all-to-all-start = ((bf16[8,64,1024]{2,1,0:T(8,128)(2,1)}), bf16[8,64,1024]{2,1,0:T(8,128)(2,1)}, u32[]{:S(2)}, u32[]{:S(2)}) async-start(bf16[8,64,1024]{2,1,0:T(8,128)(2,1)} %get-tuple-element.34), calls=%async_computation | async-start | bytes 2097152 | tf_op jit(solution)/shard_map/all_to_all | solution.py:461
  22.2 100.2 %all-gather.7.cloned.1.call-start = ((), (), s32[]{:S(2)}) async-start(), calls=%async_computation.2 | async-start | bytes 5242880 | tf_op jit(solution)/shard_map/all_gather | solution.py:470
  22.3 23.9 %collective-permute-start = (bf16[512,512]{1,0:T(8,128)(2,1)S(1)}, bf16[512,512]{1,0:T(8,128)(2,1)S(1)}, u32[]{:S(2)}, u32[]{:S(2)}) collective-permute-start(bf16[512,512]{1,0:T(8,128)(2,1)S(1)} %copy-done), channel_id=1, source_target_pairs={{0,2},{2,0},{1,3},{3,1},{4,6},{6,4},{5,7},{7,5},{8,10},{10,8},{9,1... | collective-permute-start | bytes 1572872 | tf_op jit(solution)/shard_map/ppermute | solution.py:445
  23.8 22.5 %collective-permute-start.1 = (bf16[512,512]{1,0:T(8,128)(2,1)S(1)}, bf16[512,512]{1,0:T(8,128)(2,1)S(1)}, u32[]{:S(2)}, u32[]{:S(2)}) collective-permute-start(bf16[512,512]{1,0:T(8,128)(2,1)S(1)} %copy-done), channel_id=1, source_target_pairs={{0,12},{4,0},{8,4},{12,8},{1,13},{5,1},{9,5},{13,9},{2,14},{6,2},{... | collective-permute-start | bytes 1572872 | tf_op jit(solution)/shard_map/ppermute | solution.py:445
  26.2 21.2 %collective-permute-start.2 = (bf16[512,512]{1,0:T(8,128)(2,1)S(1)}, bf16[512,512]{1,0:T(8,128)(2,1)S(1)}, u32[]{:S(2)}, u32[]{:S(2)}) collective-permute-start(bf16[512,512]{1,0:T(8,128)(2,1)S(1)} %copy-done), channel_id=1, source_target_pairs={{0,4},{4,8},{8,12},{12,0},{1,5},{5,9},{9,13},{13,1},{2,6},{6,10},{... | collective-permute-start | bytes 1572872 | tf_op jit(solution)/shard_map/ppermute | solution.py:445
  47.4 109.9 %all-gather.5.cloned.1.call-start = ((), (), s32[]{:S(2)}) async-start(), calls=%async_computation.1 | async-start | bytes 5242880 | tf_op jit(solution)/shard_map/all_gather | solution.py:471
  47.4 11.6 %collective-permute-start.12 = (bf16[512,512]{1,0:T(8,128)(2,1)S(1)}, bf16[512,512]{1,0:T(8,128)(2,1)S(1)}, u32[]{:S(2)}, u32[]{:S(2)}) collective-permute-start(bf16[512,512]{1,0:T(8,128)(2,1)S(1)} %collective-permute-done.refs_4_), channel_id=1, source_target_pairs={{0,12},{4,0},{8,4},{12,8},{1,13},{5,1},{9,5},{13,9},{2,14},{6,2},{... | collective-permute-start | bytes 1572872 | tf_op jit(solution)/shard_map/ppermute | solution.py:445
  49.1 13.5 %collective-permute-start.5 = (bf16[512,512]{1,0:T(8,128)(2,1)S(1)}, bf16[512,512]{1,0:T(8,128)(2,1)S(1)}, u32[]{:S(2)}, u32[]{:S(2)}) collective-permute-start(bf16[512,512]{1,0:T(8,128)(2,1)S(1)} %bitcast.14), channel_id=1, source_target_pairs={{0,2},{2,16},{16,18},{18,0},{1,3},{3,17},{17,19},{19,1},{4,6},{6,2... | collective-permute-start | bytes 1572872 | tf_op jit(solution)/shard_map/ppermute | solution.py:445
  50.1 13.4 %collective-permute-start.6 = (bf16[512,512]{1,0:T(8,128)(2,1)S(1)}, bf16[512,512]{1,0:T(8,128)(2,1)S(1)}, u32[]{:S(2)}, u32[]{:S(2)}) collective-permute-start(bf16[512,512]{1,0:T(8,128)(2,1)S(1)} %bitcast.13), channel_id=1, source_target_pairs={{0,18},{2,0},{16,2},{18,16},{1,19},{3,1},{17,3},{19,17},{4,22},{6,... | collective-permute-start | bytes 1572872 | tf_op jit(solution)/shard_map/ppermute | solution.py:445
  52.2 15.8 %collective-permute-start.13 = (bf16[512,512]{1,0:T(8,128)(2,1)S(1)}, bf16[512,512]{1,0:T(8,128)(2,1)S(1)}, u32[]{:S(2)}, u32[]{:S(2)}) collective-permute-start(bf16[512,512]{1,0:T(8,128)(2,1)S(1)} %collective-permute-done.refs_4_), channel_id=1, source_target_pairs={{0,4},{4,8},{8,12},{12,0},{1,5},{5,9},{9,13},{13,1},{2,6},{6,10},{... | collective-permute-start | bytes 1572872 | tf_op jit(solution)/shard_map/ppermute | solution.py:445
  53.4 22.9 %collective-permute-start.11 = (bf16[512,512]{1,0:T(8,128)(2,1)S(1)}, bf16[512,512]{1,0:T(8,128)(2,1)S(1)}, u32[]{:S(2)}, u32[]{:S(2)}) collective-permute-start(bf16[512,512]{1,0:T(8,128)(2,1)S(1)} %collective-permute-done.2.refs_2_), channel_id=1, source_target_pairs={{0,4},{4,8},{8,12},{12,0},{1,5},{5,9},{9,13},{13,1},{2,6},{6,10},{... | collective-permute-start | bytes 1572872 | tf_op jit(solution)/shard_map/ppermute | solution.py:445
  59.0 17.2 %collective-permute-start.14 = (bf16[512,512]{1,0:T(8,128)(2,1)S(1)}, bf16[512,512]{1,0:T(8,128)(2,1)S(1)}, u32[]{:S(2)}, u32[]{:S(2)}) collective-permute-start(bf16[512,512]{1,0:T(8,128)(2,1)S(1)} %collective-permute-done.12.refs_5_), channel_id=1, source_target_pairs={{0,12},{4,0},{8,4},{12,8},{1,13},{5,1},{9,5},{13,9},{2,14},{6,2},{... | collective-permute-start | bytes 1572872 | tf_op jit(solution)/shard_map/ppermute | solution.py:445
  64.3 29.1 %collective-permute-start.7 = (bf16[1024,512]{1,0:T(8,128)(2,1)}, bf16[1024,512]{1,0:T(8,128)(2,1)}, u32[]{:S(2)}, u32[]{:S(2)}) collective-permute-start(bf16[1024,512]{1,0:T(8,128)(2,1)} %constant_dynamic-update-slice_fusion.refs_3_), channel_id=1, source_target_pairs={{0,12},{4,0},{8,4},{12,8},{1,13},{5,1},{9,5},{13,9},{2,14},{6,2},{... | collective-permute-start | bytes 3145736 | tf_op jit(solution)/shard_map/ppermute | solution.py:445
  65.6 33.0 %collective-permute-start.15 = (bf16[8,64,1024]{2,1,0:T(8,128)(2,1)}, bf16[8,64,1024]{2,1,0:T(8,128)(2,1)}, u32[]{:S(2)}, u32[]{:S(2)}) collective-permute-start(bf16[8,64,1024]{2,1,0:T(8,128)(2,1)} %all-to-all-done), channel_id=1, source_target_pairs={{0,16},{16,0},{1,17},{17,1},{2,18},{18,2},{3,19},{19,3},{4,20},{20... | collective-permute-start | bytes 3145736 | tf_op jit(solution)/shard_map/ppermute | solution.py:445
  68.0 30.6 %collective-permute-start.4 = (bf16[1024,512]{1,0:T(8,128)(2,1)}, bf16[1024,512]{1,0:T(8,128)(2,1)}, u32[]{:S(2)}, u32[]{:S(2)}) collective-permute-start(bf16[1024,512]{1,0:T(8,128)(2,1)} %bitcast.refs_0_), channel_id=1, source_target_pairs={{0,4},{4,8},{8,12},{12,0},{1,5},{5,9},{9,13},{13,1},{2,6},{6,10},{... | collective-permute-start | bytes 3145736 | tf_op jit(solution)/shard_map/ppermute | solution.py:445
  78.9 2.0 %copy-start.1 = (bf16[8,512,512]{2,1,0:T(8,128)(2,1)}, bf16[8,512,512]{2,1,0:T(8,128)(2,1)S(1)}, u32[]{:S(2)}) copy-start(bf16[8,512,512]{2,1,0:T(8,128)(2,1)S(1)} %get-tuple-element.41.refs_6_.l_ref.refs_8_) | copy-start | bytes 12582916
  80.9 19.3 %collective-permute-start.16 = (f32[512,512]{1,0:T(8,128)S(1)}, f32[512,512]{1,0:T(8,128)S(1)}, u32[]{:S(2)}, u32[]{:S(2)}) collective-permute-start(f32[512,512]{1,0:T(8,128)S(1)} %get-tuple-element.43.g0), channel_id=1, source_target_pairs={{0,1},{1,0},{2,3},{3,2},{4,5},{5,4},{6,7},{7,6},{8,9},{9,8},{10,11... | collective-permute-start | bytes 3145736 | tf_op jit(solution)/shard_map/ppermute | solution.py:445
  86.9 35.4 %collective-permute-start.8 = (bf16[1024,512]{1,0:T(8,128)(2,1)}, bf16[1024,512]{1,0:T(8,128)(2,1)}, u32[]{:S(2)}, u32[]{:S(2)}) collective-permute-start(bf16[1024,512]{1,0:T(8,128)(2,1)} %constant_dynamic-update-slice_fusion.refs_3_), channel_id=1, source_target_pairs={{0,4},{4,8},{8,12},{12,0},{1,5},{5,9},{9,13},{13,1},{2,6},{6,10},{... | collective-permute-start | bytes 3145736 | tf_op jit(solution)/shard_map/ppermute | solution.py:445
  93.4 29.0 %collective-permute-start.3 = (bf16[1024,512]{1,0:T(8,128)(2,1)}, bf16[1024,512]{1,0:T(8,128)(2,1)}, u32[]{:S(2)}, u32[]{:S(2)}) collective-permute-start(bf16[1024,512]{1,0:T(8,128)(2,1)} %bitcast.refs_0_), channel_id=1, source_target_pairs={{0,12},{4,0},{8,4},{12,8},{1,13},{5,1},{9,5},{13,9},{2,14},{6,2},{... | collective-permute-start | bytes 3145736 | tf_op jit(solution)/shard_map/ppermute | solution.py:445
  98.7 42.0 %collective-permute-start.10 = (bf16[1024,512]{1,0:T(8,128)(2,1)}, bf16[1024,512]{1,0:T(8,128)(2,1)}, u32[]{:S(2)}, u32[]{:S(2)}) collective-permute-start(bf16[1024,512]{1,0:T(8,128)(2,1)} %collective-permute-done.7.refs_4_), channel_id=1, source_target_pairs={{0,12},{4,0},{8,4},{12,8},{1,13},{5,1},{9,5},{13,9},{2,14},{6,2},{... | collective-permute-start | bytes 3145736 | tf_op jit(solution)/shard_map/ppermute | solution.py:445
  98.7 44.9 %collective-permute-start.9 = (bf16[1024,512]{1,0:T(8,128)(2,1)}, bf16[1024,512]{1,0:T(8,128)(2,1)}, u32[]{:S(2)}, u32[]{:S(2)}) collective-permute-start(bf16[1024,512]{1,0:T(8,128)(2,1)} %collective-permute-done.4.refs_2_), channel_id=1, source_target_pairs={{0,4},{4,8},{8,12},{12,0},{1,5},{5,9},{9,13},{13,1},{2,6},{6,10},{... | collective-permute-start | bytes 3145736 | tf_op jit(solution)/shard_map/ppermute | solution.py:445
  122.3 16.4 %copy-start.6 = (f32[512,512]{1,0:T(8,128)}, f32[512,512]{1,0:T(8,128)S(1)}, u32[]{:S(2)}) copy-start(f32[512,512]{1,0:T(8,128)S(1)} %chol_second.1.refs_8_.inv_ref) | copy-start | bytes 3145732
  138.7 1.0 copy-start.11
  139.7 1.0 copy-start.13
  143.6 1.6 copy-start.4
  151.4 1.3 copy-start.2
  152.7 1.4 copy-start.3
  154.1 22.7 %collective-permute-start.18 = (f32[1024,512]{1,0:T(8,128)S(1)}, f32[1024,512]{1,0:T(8,128)}, u32[]{:S(2)}, u32[]{:S(2)}) collective-permute-start(f32[1024,512]{1,0:T(8,128)S(1)} %get-tuple-element.56.rm), channel_id=1, source_target_pairs={{0,1},{1,0},{2,3},{3,2},{4,5},{5,4},{6,7},{7,6},{8,9},{9,8},{10,11... | collective-permute-start | bytes 6291464 | tf_op jit(solution)/shard_map/ppermute | solution.py:445
  157.3 1.2 copy-start.12
  158.5 1.2 copy-start.14
  159.7 17.1 %copy-start.15 = (f32[8192]{0:T(1024)S(1)}, f32[8192]{0:T(1024)}, u32[]{:S(2)}) copy-start(f32[8192]{0:T(1024)} %param.3) | copy-start | bytes 98308
  175.3 1.0 copy-start.9
  176.3 8.4 %collective-permute-start.17 = (f32[1024,512]{1,0:T(8,128)}, f32[1024,512]{1,0:T(8,128)}, u32[]{:S(2)}, u32[]{:S(2)}) collective-permute-start(f32[1024,512]{1,0:T(8,128)} %get-tuple-element.55), channel_id=1, source_target_pairs={{0,1},{1,0},{2,3},{3,2},{4,5},{5,4},{6,7},{7,6},{8,9},{9,8},{10,11... | collective-permute-start | bytes 6291464 | tf_op jit(solution)/shard_map/ppermute | solution.py:445
  176.3 8.4 %collective-permute-start.19 = (f32[512,512]{1,0:T(8,128)S(1)}, f32[512,512]{1,0:T(8,128)}, u32[]{:S(2)}, u32[]{:S(2)}) collective-permute-start(f32[512,512]{1,0:T(8,128)S(1)} %get-tuple-element.58), channel_id=1, source_target_pairs={{0,1},{1,0},{2,3},{3,2},{4,5},{5,4},{6,7},{7,6},{8,9},{9,8},{10,11... | collective-permute-start | bytes 3145736 | tf_op jit(solution)/shard_map/ppermute | solution.py:445
  176.8 7.8 %copy-start.5 = (f32[1024,512]{1,0:T(8,128)S(1)}, f32[1024,512]{1,0:T(8,128)}, u32[]{:S(2)}) copy-start(f32[1024,512]{1,0:T(8,128)} %get-tuple-element.54.tm) | copy-start | bytes 6291460
  176.8 1.4 copy-start.7
  178.2 6.4 %copy-start.8 = (f32[512,512]{1,0:T(8,128)S(1)}, f32[512,512]{1,0:T(8,128)}, u32[]{:S(2)}) copy-start(f32[512,512]{1,0:T(8,128)} %copy-done.6) | copy-start | bytes 3145732
  178.2 6.5 %copy-start.10 = (f32[512,512]{1,0:T(8,128)S(1)}, f32[512,512]{1,0:T(8,128)}, u32[]{:S(2)}) copy-start(f32[512,512]{1,0:T(8,128)} %copy-done.9) | copy-start | bytes 3145732
Sparse Core Ops, SparseCore 0:
  47.5 50.5 all-gather.6
  100.3 52.5 all-gather.4

commit v3 on v2

--- a/solution.py
+++ b/solution.py
@@ -232,6 +232,10 @@
         c.wait()
 
 
+def other_zh():
+    return lax.rem(lax.axis_index("zh") + 1, 2)
+
+
 def half_lanes(dz):
     zh = lax.rem(lax.axis_index("zh") + dz, 2)
     return pl.ds(pl.multiple_of(zh * 256, 256), 256)
@@ -287,33 +291,32 @@
     rl[...] = side_products(a_in, NEAR, l_ref)
 
 
-def middle_kernel(a0, a1, l_ref, far_ref, own0, other0, rl0, own, other, rl):
-    lanes = half_lanes(0)
-    tile = nn(a0[:, lanes], far_ref[0]) + nn(a1[:, lanes], far_ref[1])
-    own[...] = own0[...] + tile[:, :512]
-    other[...] = other0[...] + tile[:, 512:]
+def middle_kernel(a0, a1, l_ref, rl0, rl):
     rl[...] = rl0[...] + side_products((a0, a1), FAR, l_ref)
 
 
 def second_kernel(*refs):
-    a_in, l_ref, b_ref = refs[:8], refs[8], refs[9]
-    own0, other0, lc_own0, lc_other0 = refs[10:14]
-    own, other, lc_own, lc_other, b_s, sems = refs[14:]
-    lanes = half_lanes(1)
+    near_in, far_in, l_ref, b_ref, far_ref = refs[:6], refs[6:8], refs[8], refs[9], refs[10]
+    own0, other0, lc_own0, lc_other0 = refs[11:15]
+    own, other, lc_own, lc_other, b_s, sems = refs[15:]
+    half = slice(None)
 
     @pl.when(pl.program_id(0) == 0)
     def _():
         fetch(b_ref, b_s, sems)
 
         def step(m, _):
-            rows, total = lead_products(l_ref, b_s, lanes, m)
+            rows, total = lead_products(l_ref, b_s, half, m)
             lc_own[rows, :] = lc_own0[rows, :] + total[:, :512]
             lc_other[rows, :] = lc_other0[rows, :] + total[:, 512:]
             return 0
 
         lax.fori_loop(0, 2, step, 0)
 
-    tile = row_products(a_in, NEAR + FAR, b_s, lanes)
+    tile = row_products(near_in, NEAR, b_s, half)
+    tile = tile + row_products(far_in, FAR, b_s, half_lanes(1))
+    for dz in range(2):
+        tile = tile + nn(far_in[dz][:, half_lanes(0)], far_ref[dz])
     own[...] = own0[...] + tile[:, :512]
     other[...] = other0[...] + tile[:, 512:]
 
@@ -340,25 +343,26 @@
     )(*a, lead, b, after)
 
 
-def gram_middle(a, lead, far, own, other, rl):
+def gram_middle(a, lead, rl):
     return pl.pallas_call(
         middle_kernel,
         grid=(4,),
-        in_specs=[BLOCK] * 2 + [once(8, 512, 512), once(2, 256, 1024)] + [BLOCK] * 3,
-        out_specs=[BLOCK] * 3,
-        out_shape=[TALL] * 3,
+        in_specs=[BLOCK] * 2 + [once(8, 512, 512)] + [BLOCK],
+        out_specs=BLOCK,
+        out_shape=TALL,
         compiler_params=params(40),
         cost_estimate=cost(5),
         name="gram_middle",
-    )(*a, lead, far, own, other, rl)
-
-
-def gram_second(a, lead, b, own, other, lc_own, lc_other):
+    )(*a, lead, rl)
+
+
+def gram_second(near_a, far_a, lead, b, b_part, own, other, lc_own, lc_other):
     return pl.pallas_call(
         second_kernel,
         grid=(4,),
-        in_specs=[BLOCK] * 8
-        + [once(8, 512, 512), ANY]
+        in_specs=[pl.BlockSpec((256, 256), lambda m: (m, other_zh()))] * 6
+        + [BLOCK] * 2
+        + [pl.BlockSpec((8, 512, 256), lambda m: (0, 0, other_zh())), ANY, once(2, 256, 1024)]
         + [BLOCK] * 2
         + [once(512, 512)] * 2,
         out_specs=[BLOCK] * 2 + [once(512, 512)] * 2,
@@ -367,7 +371,7 @@
         compiler_params=params(40),
         cost_estimate=cost(10),
         name="gram_second",
-    )(*a, lead, b, own, other, lc_own, lc_other)
+    )(*near_a, *far_a, lead, b, b_part, own, other, lc_own, lc_other)
 
 
 def column_of(lane):
@@ -480,10 +484,11 @@
 
     a = [rows, a_up, a_down, rows_z, az_up, az_down]
     own, other, rl, lc_own, lc_other, b_part = gram_first(a, lead_all, b_own, inv)
-    own, other, rl = gram_middle([a_far, az_far], lead_all, b_part, own, other, rl)
+    rl = gram_middle([a_far, az_far], lead_all, rl)
     p = panel(rl, shift(rl, "core", 1), inv, sl)
-    a = [*a, a_far, az_far]
-    own, other, lc_own, lc_other = gram_second(a, lead_all, b_z, own, other, lc_own, lc_other)
+    own, other, lc_own, lc_other = gram_second(
+        a, [a_far, az_far], lead_all, b_z, b_part, own, other, lc_own, lc_other
+    )
     sc = lax.dynamic_slice(shrink.reshape(2, 16, 256), (0, 2 * k + core, 0), (2, 1, 256))
     sc = sc.reshape(1, 512)
     out = final(own, shift(other, "core", 1), p, lc_own, shift(lc_other, "core", 1), inv, sc)

time: 202 us -> 199 us (0.985)
  Pallas kernels: 88.1 us -> 85.3 us
    pallas_call x1, Pallas kernels: 6.17 us -> 3.57 us  [gram_middle(): pl.pallas_call(middle_kernel, grid=(4,), in_specs=[BLOCK] * 2 + [once(8,...]
    unnamed x37 -> x41, local copies, waits for them, and re-layouts: 13.9 us -> 12.8 us
where the time goes in v3:
time: 199 us; the launch traced here: 198 us
  Pallas kernels  85.3 us (43%)
  waiting for transfers between devices  45.5 us (23%)
  starting transfers between devices  39.2 us (20%)
  local copies, waits for them, and re-layouts  14.3 us (7%)
  between operations  13.7 us (7%)
    ppermute x20, waiting for transfers between devices, shift(): return lax.ppermute(v, axis, [(i, (i + by) % n) for i in range(n)])  45.5 us
    ppermute x20, starting transfers between devices, shift(): return lax.ppermute(v, axis, [(i, (i + by) % n) for i in range(n)])  32.7 us
    pallas_call x1, Pallas kernels, gram_first(): pl.pallas_call(first_kernel, grid=(4,), in_specs=[BLOCK] * 6 + [once(8, 5...  16.8 us
    pallas_call x1, Pallas kernels, gram_second(): pl.pallas_call(second_kernel, grid=(4,), in_specs=[pl.BlockSpec((256, 256...  15 us
    unnamed x41, local copies, waits for them, and re-layouts  12.8 us
    pallas_call x1, Pallas kernels, chol_half(): pl.pallas_call(chol_first, in_specs=[VM] * 3, out_specs=[VM, VM], out_sha...  11.3 us
    pallas_call x1, Pallas kernels, chol_rest(): pl.pallas_call(chol_second, in_specs=[VM, VM], out_specs=VM, out_shape=SQ...  10.8 us
    pallas_call x1, Pallas kernels, final(): pl.pallas_call(final_kernel, grid=(4,), in_specs=[BLOCK] * 3 + [once(512,...  9.54 us
  transfers between devices with their start and end apart: 23, of which 9 were waited for; matrix products, arithmetic and copies ran while one was open for 1% of the time, Pallas kernels for 34%

profile of v3, /device:TPU:1, one launch (start us, length us, event | category | flops | bytes accessed | tf_op | source)
XLA Modules:
  0.0 198.0 jit_solution(5530906184655002130)
XLA Ops:
  6.5 9.3 %prep.1 = (bf16[2,8,64,512]{3,2,1,0:T(8,128)(2,1)}, bf16[8,64,512]{2,1,0:T(8,128)(2,1)}, bf16[8,64,512]{2,1,0:T(8,128)(2,1)}, bf16[512,512]{1,0:T(8,128)(2,1)}, bf16[8,64,1024]{2,1,0:T(8,128)(2,1)}) custom-call(bf16[512,8192]{1,0:T(8,128)(2,1)} %hi_ref.1, bf16[512,8192]{1,0:T(8,128)(2,1)} %hi_ref.1), custom_call_target="tpu_custom_call" | custom-call | flops 9663676416 | bytes 65536 | tf_op jit(solution)/shard_map/prep/pallas_call | solution.py:70
  15.9 6.3 %all-to-all-start = ((bf16[8,64,1024]{2,1,0:T(8,128)(2,1)}), bf16[8,64,1024]{2,1,0:T(8,128)(2,1)}, u32[]{:S(2)}, u32[]{:S(2)}) async-start(bf16[8,64,1024]{2,1,0:T(8,128)(2,1)} %get-tuple-element.31), calls=%async_computation | async-start | bytes 2097152 | tf_op jit(solution)/shard_map/all_to_all | solution.py:465
  22.3 1.5 collective-permute-start
  23.8 2.4 %collective-permute-start.1 = (bf16[512,512]{1,0:T(8,128)(2,1)S(1)}, bf16[512,512]{1,0:T(8,128)(2,1)S(1)}, u32[]{:S(2)}, u32[]{:S(2)}) collective-permute-start(bf16[512,512]{1,0:T(8,128)(2,1)S(1)} %copy-done), channel_id=1, source_target_pairs={{0,12},{4,0},{8,4},{12,8},{1,13},{5,1},{9,5},{13,9},{2,14},{6,2},{... | collective-permute-start | bytes 1572872 | tf_op jit(solution)/shard_map/ppermute | solution.py:449
  26.2 20.0 %collective-permute-done.refs_4_ = bf16[512,512]{1,0:T(8,128)(2,1)S(1)} collective-permute-done((bf16[512,512]{1,0:T(8,128)(2,1)S(1)}, bf16[512,512]{1,0:T(8,128)(2,1)S(1)}, u32[]{:S(2)}, u32[]{:S(2)}) %collective-permute-start) | collective-permute-done | bytes 524320 | tf_op jit(solution)/shard_map/ppermute | solution.py:449
  46.1 0.1 collective-permute-done.1.refs_1_
  46.3 1.1 collective-permute-done.2.refs_2_
  47.4 0.0 all-gather.5.cloned.1.call-start
  47.4 1.7 collective-permute-start.12
  49.1 0.9 collective-permute-start.5
  50.0 2.2 %collective-permute-start.6 = (bf16[512,512]{1,0:T(8,128)(2,1)S(1)}, bf16[512,512]{1,0:T(8,128)(2,1)S(1)}, u32[]{:S(2)}, u32[]{:S(2)}) collective-permute-start(bf16[512,512]{1,0:T(8,128)(2,1)S(1)} %bitcast.13), channel_id=1, source_target_pairs={{0,18},{2,0},{16,2},{18,16},{1,19},{3,1},{17,3},{19,17},{4,22},{6,... | collective-permute-start | bytes 1572872 | tf_op jit(solution)/shard_map/ppermute | solution.py:449
  52.2 1.1 collective-permute-start.13
  53.4 5.6 %collective-permute-done.12.refs_5_ = bf16[512,512]{1,0:T(8,128)(2,1)S(1)} collective-permute-done((bf16[512,512]{1,0:T(8,128)(2,1)S(1)}, bf16[512,512]{1,0:T(8,128)(2,1)S(1)}, u32[]{:S(2)}, u32[]{:S(2)}) %collective-permute-start.12) | collective-permute-done | bytes 524320 | tf_op jit(solution)/shard_map/ppermute | solution.py:449
  59.0 3.1 %collective-permute-start.14 = (bf16[512,512]{1,0:T(8,128)(2,1)S(1)}, bf16[512,512]{1,0:T(8,128)(2,1)S(1)}, u32[]{:S(2)}, u32[]{:S(2)}) collective-permute-start(bf16[512,512]{1,0:T(8,128)(2,1)S(1)} %collective-permute-done.12.refs_5_), channel_id=1, source_target_pairs={{0,12},{4,0},{8,4},{12,8},{1,13},{5,1},{9,5},{13,9},{2,14},{6,2},{... | collective-permute-start | bytes 1572872 | tf_op jit(solution)/shard_map/ppermute | solution.py:449
  62.1 0.5 collective-permute-done.5
  62.6 0.8 constant_dynamic-update-slice_fusion.1
  63.4 0.8 constant_dynamic-update-slice_fusion.refs_3_
  64.3 1.4 collective-permute-start.7
  65.6 2.4 %collective-permute-start.15 = (bf16[8,64,1024]{2,1,0:T(8,128)(2,1)}, bf16[8,64,1024]{2,1,0:T(8,128)(2,1)}, u32[]{:S(2)}, u32[]{:S(2)}) collective-permute-start(bf16[8,64,1024]{2,1,0:T(8,128)(2,1)} %all-to-all-done), channel_id=1, source_target_pairs={{0,16},{16,0},{1,17},{17,1},{2,18},{18,2},{3,19},{19,3},{4,20},{20... | collective-permute-start | bytes 3145736 | tf_op jit(solution)/shard_map/ppermute | solution.py:449
  68.0 0.5 collective-permute-start.4
  68.5 7.7 %collective-permute-done.11.refs_3_ = bf16[512,512]{1,0:T(8,128)(2,1)S(1)} collective-permute-done((bf16[512,512]{1,0:T(8,128)(2,1)S(1)}, bf16[512,512]{1,0:T(8,128)(2,1)S(1)}, u32[]{:S(2)}, u32[]{:S(2)}) %collective-permute-start.11) | collective-permute-done | bytes 524320 | tf_op jit(solution)/shard_map/ppermute | solution.py:449
  76.2 2.6 %lead_gram.1 = (f32[512,512]{1,0:T(8,128)S(1)}, bf16[8,512,512]{2,1,0:T(8,128)(2,1)S(1)}) custom-call(bf16[512,512]{1,0:T(8,128)(2,1)S(1)} %copy-done, bf16[512,512]{1,0:T(8,128)(2,1)S(1)} %collective-permute-done.1.refs_1_, bf16[512,512]{1,0:T(8,128)(2,1)S(1)} %collective-permute-done.2.refs_2_, bf16[512,512]{1,0:T(8,128)(2,1)S(1)} %collective-permute-done.11.refs_3_, ...), custom_call_target="tpu_custom_call" | custom-call | flops 4294967296 | bytes 65536 | tf_op jit(solution)/shard_map/lead_gram/pallas_call | solution.py:117
  78.9 2.0 %copy-done.1 = bf16[8,512,512]{2,1,0:T(8,128)(2,1)} copy-done((bf16[8,512,512]{2,1,0:T(8,128)(2,1)}, bf16[8,512,512]{2,1,0:T(8,128)(2,1)S(1)}, u32[]{:S(2)}) %copy-start.1) | copy-done | bytes 4194328
  80.9 5.4 %collective-permute-start.16 = (f32[512,512]{1,0:T(8,128)S(1)}, f32[512,512]{1,0:T(8,128)S(1)}, u32[]{:S(2)}, u32[]{:S(2)}) collective-permute-start(f32[512,512]{1,0:T(8,128)S(1)} %get-tuple-element.40.g0), channel_id=1, source_target_pairs={{0,1},{1,0},{2,3},{3,2},{4,5},{5,4},{6,7},{7,6},{8,9},{9,8},{10,11... | collective-permute-start | bytes 3145736 | tf_op jit(solution)/shard_map/ppermute | solution.py:449
  86.2 0.7 slice.3
  86.9 6.4 %collective-permute-done.7.refs_4_ = bf16[1024,512]{1,0:T(8,128)(2,1)} collective-permute-done((bf16[1024,512]{1,0:T(8,128)(2,1)}, bf16[1024,512]{1,0:T(8,128)(2,1)}, u32[]{:S(2)}, u32[]{:S(2)}) %collective-permute-start.7) | collective-permute-done | bytes 1048608 | tf_op jit(solution)/shard_map/ppermute | solution.py:449
  93.4 3.4 %collective-permute-start.3 = (bf16[1024,512]{1,0:T(8,128)(2,1)}, bf16[1024,512]{1,0:T(8,128)(2,1)}, u32[]{:S(2)}, u32[]{:S(2)}) collective-permute-start(bf16[1024,512]{1,0:T(8,128)(2,1)} %bitcast.refs_0_), channel_id=1, source_target_pairs={{0,12},{4,0},{8,4},{12,8},{1,13},{5,1},{9,5},{13,9},{2,14},{6,2},{... | collective-permute-start | bytes 3145736 | tf_op jit(solution)/shard_map/ppermute | solution.py:449
  96.8 1.9 collective-permute-done.4.refs_2_
  98.7 1.5 collective-permute-start.9
  100.2 11.3 %chol_first.1 = (f32[512,512]{1,0:T(8,128)S(1)}, f32[512,512]{1,0:T(8,128)S(1)}) custom-call(f32[512,512]{1,0:T(8,128)S(1)} %get-tuple-element.40.g0, f32[512,512]{1,0:T(8,128)S(1)} %collective-permute-done.16.g1, f32[1,512]{1,0:T(1,128)S(1)} %bitcast.8), custom_call_target="tpu_custom_call" | custom-call | flops 85899345920 | bytes 65536 | tf_op jit(solution)/shard_map/chol_first/pallas_call | solution.py:196
  111.5 10.8 %chol_second.1.refs_8_.inv_ref = f32[512,512]{1,0:T(8,128)S(1)} custom-call(f32[512,512]{1,0:T(8,128)S(1)} %get-tuple-element.41.a0, f32[512,512]{1,0:T(8,128)S(1)} %get-tuple-element.42.i0), custom_call_target="tpu_custom_call" | custom-call | flops 85899345920 | bytes 65536 | tf_op jit(solution)/shard_map/chol_second/pallas_call | solution.py:208
  122.4 16.8 %gram_first.1 = (f32[1024,512]{1,0:T(8,128)S(1)}, f32[1024,512]{1,0:T(8,128)}, f32[1024,512]{1,0:T(8,128)}, f32[512,512]{1,0:T(8,128)S(1)}, f32[512,512]{1,0:T(8,128)S(1)}, /*index=5*/bf16[2,256,1024]{2,1,0:T(8,128)(2,1)S(1)}) custom-call(bf16[1024,512]{1,0:T(8,128)(2,1)} %bitcast.refs_0_, bf16[1024,512]{1,0:T(8,128)(2,1)} %collective-permute-done.3.refs_1_, ...), custom_call_target="tpu_custom_call" | custom-call | flops 18253611008 | bytes 65536 | tf_op jit(solution)/shard_map/gram_first/pallas_call | solution.py:333
  139.2 1.3 copy-done.5
  140.5 1.0 copy-done.13
  141.5 2.1 %collective-permute-done.9.refs_6_.a0 = bf16[1024,512]{1,0:T(8,128)(2,1)} collective-permute-done((bf16[1024,512]{1,0:T(8,128)(2,1)}, bf16[1024,512]{1,0:T(8,128)(2,1)}, u32[]{:S(2)}, u32[]{:S(2)}) %collective-permute-start.9) | collective-permute-done | bytes 1048608 | tf_op jit(solution)/shard_map/ppermute | solution.py:449
  143.6 1.6 copy-done.3
  145.2 3.6 %gram_middle.1.rm = f32[1024,512]{1,0:T(8,128)S(1)} custom-call(bf16[1024,512]{1,0:T(8,128)(2,1)} %collective-permute-done.9.refs_6_.a0, bf16[1024,512]{1,0:T(8,128)(2,1)} %collective-permute-done.10.refs_7_.a1, bf16[8,512,512]{2,1,0:T(8,128)(2,1)S(1)} %copy-done.2, f32[1024,512]{1,0:T(8,128)S(1)} %copy-done.3), custom_call_target="tpu_custom_call" | custom-call | flops 5368709120 | bytes 65536 | tf_op jit(solution)/shard_map/gram_middle/pallas_call | solution.py:347
  148.8 4.8 %collective-permute-start.18 = (f32[1024,512]{1,0:T(8,128)S(1)}, f32[1024,512]{1,0:T(8,128)}, u32[]{:S(2)}, u32[]{:S(2)}) collective-permute-start(f32[1024,512]{1,0:T(8,128)S(1)} %gram_middle.1.rm), channel_id=1, source_target_pairs={{0,1},{1,0},{2,3},{3,2},{4,5},{5,4},{6,7},{7,6},{8,9},{9,8},{10,11... | collective-permute-start | bytes 6291464 | tf_op jit(solution)/shard_map/ppermute | solution.py:449
  153.6 1.2 copy-done.12
  154.8 1.2 copy-done.14
  156.0 1.2 copy-done.16
  157.3 15.0 %gram_second.1 = (f32[1024,512]{1,0:T(8,128)}, f32[1024,512]{1,0:T(8,128)}, f32[512,512]{1,0:T(8,128)S(1)}, f32[512,512]{1,0:T(8,128)S(1)}) custom-call(bf16[1024,512]{1,0:T(8,128)(2,1)} %bitcast.refs_0_, bf16[1024,512]{1,0:T(8,128)(2,1)} %collective-permute-done.3.refs_1_, bf16[1024,512]{1,0:T(8,128)(2,1)} %collective-permute-done.4.refs_2_, ...), custom_call_target="tpu_custom_call" | custom-call | flops 10737418240 | bytes 65536 | tf_op jit(solution)/shard_map/gram_second/pallas_call | solution.py:360
  172.3 1.0 copy-done.9
  173.3 0.0 collective-permute-start.17
  173.3 0.5 collective-permute-start.19
  173.8 1.4 copy-done.7
  175.2 6.4 %panel.1.p_ref = f32[1024,512]{1,0:T(8,128)S(1)} custom-call(f32[1024,512]{1,0:T(8,128)S(1)} %gram_middle.1.rm, f32[1024,512]{1,0:T(8,128)} %collective-permute-done.18.rr, f32[512,512]{1,0:T(8,128)S(1)} %copy-done.7, f32[1,512]{1,0:T(1,128)S(1)} %bitcast.9), custom_call_target="tpu_custom_call" | custom-call | flops 5368709120 | bytes 65536 | tf_op jit(solution)/shard_map/panel/pallas_call | solution.py:397
  181.7 9.5 %final.1 = f32[1024,1,512]{2,1,0:T(1,128)} custom-call(f32[1024,512]{1,0:T(8,128)S(1)} %copy-done.4, f32[1024,512]{1,0:T(8,128)} %collective-permute-done.17.tr, f32[1024,512]{1,0:T(8,128)S(1)} %panel.1.p_ref, f32[512,512]{1,0:T(8,128)S(1)} %copy-done.10, f32[512,512]{1,0:T(8,128)} %collective-permute-done.19.lr, f32[512,512]{1,0:T(8,128)S(1)} %copy-done.8, ...), custom_call_target="tpu_custom_call" | custom-call | flops 9663676416 | bytes 65536 | tf_op jit(solution)/shard_map/final/pallas_call | solution.py:434
  (54 shorter events, 0.2 us)
Async XLA Ops:
  15.8 6.4 %copy-start = (bf16[512,512]{1,0:T(8,128)(2,1)S(1)}, bf16[512,512]{1,0:T(8,128)(2,1)}, u32[]{:S(2)}) copy-start(bf16[512,512]{1,0:T(8,128)(2,1)} %get-tuple-element.30.refs_0_) | copy-start | bytes 1572868
  15.8 33.3 %copy-start.19 = (bf16[8,64,512]{2,1,0:T(8,128)(2,1)S(1)}, bf16[8,64,512]{2,1,0:T(8,128)(2,1)}, u32[]{:S(2)}) copy-start(bf16[8,64,512]{2,1,0:T(8,128)(2,1)} %get-tuple-element.34) | copy-start | bytes 1572868
  15.9 34.2 %copy-start.18 = (bf16[8,64,512]{2,1,0:T(8,128)(2,1)S(1)}, bf16[8,64,512]{2,1,0:T(8,128)(2,1)}, u32[]{:S(2)}) copy-start(bf16[8,64,512]{2,1,0:T(8,128)(2,1)} %get-tuple-element.35) | copy-start | bytes 1572868
  15.9 31.5 %all-to-all-start = ((bf16[8,64,1024]{2,1,0:T(8,128)(2,1)}), bf16[8,64,1024]{2,1,0:T(8,128)(2,1)}, u32[]{:S(2)}, u32[]{:S(2)}) async-start(bf16[8,64,1024]{2,1,0:T(8,128)(2,1)} %get-tuple-element.31), calls=%async_computation | async-start | bytes 2097152 | tf_op jit(solution)/shard_map/all_to_all | solution.py:465
  22.2 100.2 %all-gather.7.cloned.1.call-start = ((), (), s32[]{:S(2)}) async-start(), calls=%async_computation.2 | async-start | bytes 5242880 | tf_op jit(solution)/shard_map/all_gather | solution.py:474
  22.3 23.9 %collective-permute-start = (bf16[512,512]{1,0:T(8,128)(2,1)S(1)}, bf16[512,512]{1,0:T(8,128)(2,1)S(1)}, u32[]{:S(2)}, u32[]{:S(2)}) collective-permute-start(bf16[512,512]{1,0:T(8,128)(2,1)S(1)} %copy-done), channel_id=1, source_target_pairs={{0,2},{2,0},{1,3},{3,1},{4,6},{6,4},{5,7},{7,5},{8,10},{10,8},{9,1... | collective-permute-start | bytes 1572872 | tf_op jit(solution)/shard_map/ppermute | solution.py:449
  23.8 22.5 %collective-permute-start.1 = (bf16[512,512]{1,0:T(8,128)(2,1)S(1)}, bf16[512,512]{1,0:T(8,128)(2,1)S(1)}, u32[]{:S(2)}, u32[]{:S(2)}) collective-permute-start(bf16[512,512]{1,0:T(8,128)(2,1)S(1)} %copy-done), channel_id=1, source_target_pairs={{0,12},{4,0},{8,4},{12,8},{1,13},{5,1},{9,5},{13,9},{2,14},{6,2},{... | collective-permute-start | bytes 1572872 | tf_op jit(solution)/shard_map/ppermute | solution.py:449
  26.2 21.2 %collective-permute-start.2 = (bf16[512,512]{1,0:T(8,128)(2,1)S(1)}, bf16[512,512]{1,0:T(8,128)(2,1)S(1)}, u32[]{:S(2)}, u32[]{:S(2)}) collective-permute-start(bf16[512,512]{1,0:T(8,128)(2,1)S(1)} %copy-done), channel_id=1, source_target_pairs={{0,4},{4,8},{8,12},{12,0},{1,5},{5,9},{9,13},{13,1},{2,6},{6,10},{... | collective-permute-start | bytes 1572872 | tf_op jit(solution)/shard_map/ppermute | solution.py:449
  47.4 106.2 %all-gather.5.cloned.1.call-start = ((), (), s32[]{:S(2)}) async-start(), calls=%async_computation.1 | async-start | bytes 5242880 | tf_op jit(solution)/shard_map/all_gather | solution.py:475
  47.4 11.6 %collective-permute-start.12 = (bf16[512,512]{1,0:T(8,128)(2,1)S(1)}, bf16[512,512]{1,0:T(8,128)(2,1)S(1)}, u32[]{:S(2)}, u32[]{:S(2)}) collective-permute-start(bf16[512,512]{1,0:T(8,128)(2,1)S(1)} %collective-permute-done.refs_4_), channel_id=1, source_target_pairs={{0,12},{4,0},{8,4},{12,8},{1,13},{5,1},{9,5},{13,9},{2,14},{6,2},{... | collective-permute-start | bytes 1572872 | tf_op jit(solution)/shard_map/ppermute | solution.py:449
  49.1 13.5 %collective-permute-start.5 = (bf16[512,512]{1,0:T(8,128)(2,1)S(1)}, bf16[512,512]{1,0:T(8,128)(2,1)S(1)}, u32[]{:S(2)}, u32[]{:S(2)}) collective-permute-start(bf16[512,512]{1,0:T(8,128)(2,1)S(1)} %bitcast.14), channel_id=1, source_target_pairs={{0,2},{2,16},{16,18},{18,0},{1,3},{3,17},{17,19},{19,1},{4,6},{6,2... | collective-permute-start | bytes 1572872 | tf_op jit(solution)/shard_map/ppermute | solution.py:449
  50.0 13.4 %collective-permute-start.6 = (bf16[512,512]{1,0:T(8,128)(2,1)S(1)}, bf16[512,512]{1,0:T(8,128)(2,1)S(1)}, u32[]{:S(2)}, u32[]{:S(2)}) collective-permute-start(bf16[512,512]{1,0:T(8,128)(2,1)S(1)} %bitcast.13), channel_id=1, source_target_pairs={{0,18},{2,0},{16,2},{18,16},{1,19},{3,1},{17,3},{19,17},{4,22},{6,... | collective-permute-start | bytes 1572872 | tf_op jit(solution)/shard_map/ppermute | solution.py:449
  52.2 15.8 %collective-permute-start.13 = (bf16[512,512]{1,0:T(8,128)(2,1)S(1)}, bf16[512,512]{1,0:T(8,128)(2,1)S(1)}, u32[]{:S(2)}, u32[]{:S(2)}) collective-permute-start(bf16[512,512]{1,0:T(8,128)(2,1)S(1)} %collective-permute-done.refs_4_), channel_id=1, source_target_pairs={{0,4},{4,8},{8,12},{12,0},{1,5},{5,9},{9,13},{13,1},{2,6},{6,10},{... | collective-permute-start | bytes 1572872 | tf_op jit(solution)/shard_map/ppermute | solution.py:449
  53.3 22.9 %collective-permute-start.11 = (bf16[512,512]{1,0:T(8,128)(2,1)S(1)}, bf16[512,512]{1,0:T(8,128)(2,1)S(1)}, u32[]{:S(2)}, u32[]{:S(2)}) collective-permute-start(bf16[512,512]{1,0:T(8,128)(2,1)S(1)} %collective-permute-done.2.refs_2_), channel_id=1, source_target_pairs={{0,4},{4,8},{8,12},{12,0},{1,5},{5,9},{9,13},{13,1},{2,6},{6,10},{... | collective-permute-start | bytes 1572872 | tf_op jit(solution)/shard_map/ppermute | solution.py:449
  59.0 17.2 %collective-permute-start.14 = (bf16[512,512]{1,0:T(8,128)(2,1)S(1)}, bf16[512,512]{1,0:T(8,128)(2,1)S(1)}, u32[]{:S(2)}, u32[]{:S(2)}) collective-permute-start(bf16[512,512]{1,0:T(8,128)(2,1)S(1)} %collective-permute-done.12.refs_5_), channel_id=1, source_target_pairs={{0,12},{4,0},{8,4},{12,8},{1,13},{5,1},{9,5},{13,9},{2,14},{6,2},{... | collective-permute-start | bytes 1572872 | tf_op jit(solution)/shard_map/ppermute | solution.py:449
  64.3 29.1 %collective-permute-start.7 = (bf16[1024,512]{1,0:T(8,128)(2,1)}, bf16[1024,512]{1,0:T(8,128)(2,1)}, u32[]{:S(2)}, u32[]{:S(2)}) collective-permute-start(bf16[1024,512]{1,0:T(8,128)(2,1)} %constant_dynamic-update-slice_fusion.refs_3_), channel_id=1, source_target_pairs={{0,12},{4,0},{8,4},{12,8},{1,13},{5,1},{9,5},{13,9},{2,14},{6,2},{... | collective-permute-start | bytes 3145736 | tf_op jit(solution)/shard_map/ppermute | solution.py:449
  65.6 33.1 %collective-permute-start.15 = (bf16[8,64,1024]{2,1,0:T(8,128)(2,1)}, bf16[8,64,1024]{2,1,0:T(8,128)(2,1)}, u32[]{:S(2)}, u32[]{:S(2)}) collective-permute-start(bf16[8,64,1024]{2,1,0:T(8,128)(2,1)} %all-to-all-done), channel_id=1, source_target_pairs={{0,16},{16,0},{1,17},{17,1},{2,18},{18,2},{3,19},{19,3},{4,20},{20... | collective-permute-start | bytes 3145736 | tf_op jit(solution)/shard_map/ppermute | solution.py:449
  68.0 30.7 %collective-permute-start.4 = (bf16[1024,512]{1,0:T(8,128)(2,1)}, bf16[1024,512]{1,0:T(8,128)(2,1)}, u32[]{:S(2)}, u32[]{:S(2)}) collective-permute-start(bf16[1024,512]{1,0:T(8,128)(2,1)} %bitcast.refs_0_), channel_id=1, source_target_pairs={{0,4},{4,8},{8,12},{12,0},{1,5},{5,9},{9,13},{13,1},{2,6},{6,10},{... | collective-permute-start | bytes 3145736 | tf_op jit(solution)/shard_map/ppermute | solution.py:449
  78.8 2.0 %copy-start.1 = (bf16[8,512,512]{2,1,0:T(8,128)(2,1)}, bf16[8,512,512]{2,1,0:T(8,128)(2,1)S(1)}, u32[]{:S(2)}) copy-start(bf16[8,512,512]{2,1,0:T(8,128)(2,1)S(1)} %get-tuple-element.38.refs_6_.refs_8_.l_ref) | copy-start | bytes 12582916
  80.9 19.3 %collective-permute-start.16 = (f32[512,512]{1,0:T(8,128)S(1)}, f32[512,512]{1,0:T(8,128)S(1)}, u32[]{:S(2)}, u32[]{:S(2)}) collective-permute-start(f32[512,512]{1,0:T(8,128)S(1)} %get-tuple-element.40.g0), channel_id=1, source_target_pairs={{0,1},{1,0},{2,3},{3,2},{4,5},{5,4},{6,7},{7,6},{8,9},{9,8},{10,11... | collective-permute-start | bytes 3145736 | tf_op jit(solution)/shard_map/ppermute | solution.py:449
  86.9 35.4 %collective-permute-start.8 = (bf16[1024,512]{1,0:T(8,128)(2,1)}, bf16[1024,512]{1,0:T(8,128)(2,1)}, u32[]{:S(2)}, u32[]{:S(2)}) collective-permute-start(bf16[1024,512]{1,0:T(8,128)(2,1)} %constant_dynamic-update-slice_fusion.refs_3_), channel_id=1, source_target_pairs={{0,4},{4,8},{8,12},{12,0},{1,5},{5,9},{9,13},{13,1},{2,6},{6,10},{... | collective-permute-start | bytes 3145736 | tf_op jit(solution)/shard_map/ppermute | solution.py:449
  93.4 29.0 %collective-permute-start.3 = (bf16[1024,512]{1,0:T(8,128)(2,1)}, bf16[1024,512]{1,0:T(8,128)(2,1)}, u32[]{:S(2)}, u32[]{:S(2)}) collective-permute-start(bf16[1024,512]{1,0:T(8,128)(2,1)} %bitcast.refs_0_), channel_id=1, source_target_pairs={{0,12},{4,0},{8,4},{12,8},{1,13},{5,1},{9,5},{13,9},{2,14},{6,2},{... | collective-permute-start | bytes 3145736 | tf_op jit(solution)/shard_map/ppermute | solution.py:449
  98.7 42.8 %collective-permute-start.10 = (bf16[1024,512]{1,0:T(8,128)(2,1)}, bf16[1024,512]{1,0:T(8,128)(2,1)}, u32[]{:S(2)}, u32[]{:S(2)}) collective-permute-start(bf16[1024,512]{1,0:T(8,128)(2,1)} %collective-permute-done.7.refs_4_), channel_id=1, source_target_pairs={{0,12},{4,0},{8,4},{12,8},{1,13},{5,1},{9,5},{13,9},{2,14},{6,2},{... | collective-permute-start | bytes 3145736 | tf_op jit(solution)/shard_map/ppermute | solution.py:449
  98.7 44.9 %collective-permute-start.9 = (bf16[1024,512]{1,0:T(8,128)(2,1)}, bf16[1024,512]{1,0:T(8,128)(2,1)}, u32[]{:S(2)}, u32[]{:S(2)}) collective-permute-start(bf16[1024,512]{1,0:T(8,128)(2,1)} %collective-permute-done.4.refs_2_), channel_id=1, source_target_pairs={{0,4},{4,8},{8,12},{12,0},{1,5},{5,9},{9,13},{13,1},{2,6},{6,10},{... | collective-permute-start | bytes 3145736 | tf_op jit(solution)/shard_map/ppermute | solution.py:449
  122.3 16.8 %copy-start.6 = (f32[512,512]{1,0:T(8,128)}, f32[512,512]{1,0:T(8,128)S(1)}, u32[]{:S(2)}) copy-start(f32[512,512]{1,0:T(8,128)S(1)} %chol_second.1.refs_8_.inv_ref) | copy-start | bytes 3145732
  122.4 21.2 %copy-start.2 = (bf16[8,512,512]{2,1,0:T(8,128)(2,1)S(1)}, bf16[8,512,512]{2,1,0:T(8,128)(2,1)}, u32[]{:S(2)}) copy-start(bf16[8,512,512]{2,1,0:T(8,128)(2,1)} %copy-done.1) | copy-start | bytes 12582916
  139.2 1.3 copy-start.5
  140.5 1.0 copy-start.13
  141.5 7.3 %copy-start.11 = (f32[512,512]{1,0:T(8,128)}, f32[512,512]{1,0:T(8,128)S(1)}, u32[]{:S(2)}) copy-start(f32[512,512]{1,0:T(8,128)S(1)} %get-tuple-element.46.refs_13_) | copy-start | bytes 3145732
  141.5 7.3 %copy-start.15 = (bf16[2,256,1024]{2,1,0:T(8,128)(2,1)}, bf16[2,256,1024]{2,1,0:T(8,128)(2,1)S(1)}, u32[]{:S(2)}) copy-start(bf16[2,256,1024]{2,1,0:T(8,128)(2,1)S(1)} %get-tuple-element.43.refs_10_) | copy-start | bytes 3145732
  143.6 1.6 copy-start.3
  148.8 25.0 %collective-permute-start.18 = (f32[1024,512]{1,0:T(8,128)S(1)}, f32[1024,512]{1,0:T(8,128)}, u32[]{:S(2)}, u32[]{:S(2)}) collective-permute-start(f32[1024,512]{1,0:T(8,128)S(1)} %gram_middle.1.rm), channel_id=1, source_target_pairs={{0,1},{1,0},{2,3},{3,2},{4,5},{5,4},{6,7},{7,6},{8,9},{9,8},{10,11... | collective-permute-start | bytes 6291464 | tf_op jit(solution)/shard_map/ppermute | solution.py:449
  153.6 1.2 copy-start.12
  154.8 1.2 copy-start.14
  156.0 1.2 copy-start.16
  157.3 16.5 %copy-start.17 = (f32[8192]{0:T(1024)S(1)}, f32[8192]{0:T(1024)}, u32[]{:S(2)}) copy-start(f32[8192]{0:T(1024)} %param.3) | copy-start | bytes 98308
  172.3 1.0 copy-start.9
  173.3 8.4 %collective-permute-start.17 = (f32[1024,512]{1,0:T(8,128)}, f32[1024,512]{1,0:T(8,128)}, u32[]{:S(2)}, u32[]{:S(2)}) collective-permute-start(f32[1024,512]{1,0:T(8,128)} %get-tuple-element.49), channel_id=1, source_target_pairs={{0,1},{1,0},{2,3},{3,2},{4,5},{5,4},{6,7},{7,6},{8,9},{9,8},{10,11... | collective-permute-start | bytes 6291464 | tf_op jit(solution)/shard_map/ppermute | solution.py:449
  173.3 8.3 %collective-permute-start.19 = (f32[512,512]{1,0:T(8,128)S(1)}, f32[512,512]{1,0:T(8,128)}, u32[]{:S(2)}, u32[]{:S(2)}) collective-permute-start(f32[512,512]{1,0:T(8,128)S(1)} %get-tuple-element.52), channel_id=1, source_target_pairs={{0,1},{1,0},{2,3},{3,2},{4,5},{5,4},{6,7},{7,6},{8,9},{9,8},{10,11... | collective-permute-start | bytes 3145736 | tf_op jit(solution)/shard_map/ppermute | solution.py:449
  173.8 7.8 %copy-start.4 = (f32[1024,512]{1,0:T(8,128)S(1)}, f32[1024,512]{1,0:T(8,128)}, u32[]{:S(2)}) copy-start(f32[1024,512]{1,0:T(8,128)} %get-tuple-element.48.tm) | copy-start | bytes 6291460
  173.8 1.4 copy-start.7
  175.2 6.4 %copy-start.8 = (f32[512,512]{1,0:T(8,128)S(1)}, f32[512,512]{1,0:T(8,128)}, u32[]{:S(2)}) copy-start(f32[512,512]{1,0:T(8,128)} %copy-done.6) | copy-start | bytes 3145732
  175.2 6.5 %copy-start.10 = (f32[512,512]{1,0:T(8,128)S(1)}, f32[512,512]{1,0:T(8,128)}, u32[]{:S(2)}) copy-start(f32[512,512]{1,0:T(8,128)} %copy-done.9) | copy-start | bytes 3145732
Sparse Core Ops, SparseCore 0:
  47.5 50.5 all-gather.6
  100.3 52.4 all-gather.4

commit v4 on v3

--- a/solution.py
+++ b/solution.py
@@ -368,7 +368,7 @@
         out_specs=[BLOCK] * 2 + [once(512, 512)] * 2,
         out_shape=[TALL] * 2 + [SQUARE] * 2,
         scratch_shapes=SCRATCH,
-        compiler_params=params(40),
+        compiler_params=params(58),
         cost_estimate=cost(10),
         name="gram_second",
     )(*near_a, *far_a, lead, b, b_part, own, other, lc_own, lc_other)

time: 199 us -> 195 us (0.980)
  local copies, waits for them, and re-layouts: 14.3 us -> 9.66 us
    unnamed x41 -> x33, local copies, waits for them, and re-layouts: 12.8 us -> 8.13 us
  transfers between devices with their start and end apart: 23 -> 23, of which waited for: 9 -> 9; matrix products, arithmetic and copies ran while one was open for 1% -> 1% of each run, Pallas kernels for 34% -> 35%
where the time goes in v4:
time: 195 us; the launch traced here: 194 us
  Pallas kernels  86.1 us (44%)
  waiting for transfers between devices  45.6 us (23%)
  starting transfers between devices  39.2 us (20%)
  between operations  13.7 us (7%)
  local copies, waits for them, and re-layouts  9.66 us (5%)
    ppermute x20, waiting for transfers between devices, shift(): return lax.ppermute(v, axis, [(i, (i + by) % n) for i in range(n)])  45.5 us
    ppermute x20, starting transfers between devices, shift(): return lax.ppermute(v, axis, [(i, (i + by) % n) for i in range(n)])  32.8 us
    pallas_call x1, Pallas kernels, gram_first(): pl.pallas_call(first_kernel, grid=(4,), in_specs=[BLOCK] * 6 + [once(8, 5...  16.8 us
    pallas_call x1, Pallas kernels, gram_second(): pl.pallas_call(second_kernel, grid=(4,), in_specs=[pl.BlockSpec((256, 256...  16.1 us
    pallas_call x1, Pallas kernels, chol_half(): pl.pallas_call(chol_first, in_specs=[VM] * 3, out_specs=[VM, VM], out_sha...  11.3 us
    pallas_call x1, Pallas kernels, chol_rest(): pl.pallas_call(chol_second, in_specs=[VM, VM], out_specs=VM, out_shape=SQ...  10.8 us
    pallas_call x1, Pallas kernels, prep(): pl.pallas_call(prep_kernel, grid=(8,), in_specs=[pl.BlockSpec((ROWS, 512)...  9.3 us
    pallas_call x1, Pallas kernels, final(): pl.pallas_call(final_kernel, grid=(4,), in_specs=[BLOCK] * 3 + [once(512,...  9.18 us
  transfers between devices with their start and end apart: 23, of which 9 were waited for; matrix products, arithmetic and copies ran while one was open for 1% of the time, Pallas kernels for 35%

profile of v4, /device:TPU:1, one launch (start us, length us, event | category | flops | bytes accessed | tf_op | source)
XLA Modules:
  0.0 194.2 jit_solution(10471179142777597570)
XLA Ops:
  6.5 9.3 %prep.1 = (bf16[2,8,64,512]{3,2,1,0:T(8,128)(2,1)}, bf16[8,64,512]{2,1,0:T(8,128)(2,1)}, bf16[8,64,512]{2,1,0:T(8,128)(2,1)}, bf16[512,512]{1,0:T(8,128)(2,1)}, bf16[8,64,1024]{2,1,0:T(8,128)(2,1)}) custom-call(bf16[512,8192]{1,0:T(8,128)(2,1)} %hi_ref.1, bf16[512,8192]{1,0:T(8,128)(2,1)} %hi_ref.1), custom_call_target="tpu_custom_call" | custom-call | flops 9663676416 | bytes 65536 | tf_op jit(solution)/shard_map/prep/pallas_call | solution.py:70
  15.9 6.3 %all-to-all-start = ((bf16[8,64,1024]{2,1,0:T(8,128)(2,1)}), bf16[8,64,1024]{2,1,0:T(8,128)(2,1)}, u32[]{:S(2)}, u32[]{:S(2)}) async-start(bf16[8,64,1024]{2,1,0:T(8,128)(2,1)} %get-tuple-element.31), calls=%async_computation | async-start | bytes 2097152 | tf_op jit(solution)/shard_map/all_to_all | solution.py:465
  22.2 0.0 all-gather.7.cloned.1.call-start
  22.3 1.5 collective-permute-start
  23.8 2.4 %collective-permute-start.1 = (bf16[512,512]{1,0:T(8,128)(2,1)S(1)}, bf16[512,512]{1,0:T(8,128)(2,1)S(1)}, u32[]{:S(2)}, u32[]{:S(2)}) collective-permute-start(bf16[512,512]{1,0:T(8,128)(2,1)S(1)} %copy-done), channel_id=1, source_target_pairs={{0,12},{4,0},{8,4},{12,8},{1,13},{5,1},{9,5},{13,9},{2,14},{6,2},{... | collective-permute-start | bytes 1572872 | tf_op jit(solution)/shard_map/ppermute | solution.py:449
  26.2 20.0 %collective-permute-done.refs_4_ = bf16[512,512]{1,0:T(8,128)(2,1)S(1)} collective-permute-done((bf16[512,512]{1,0:T(8,128)(2,1)S(1)}, bf16[512,512]{1,0:T(8,128)(2,1)S(1)}, u32[]{:S(2)}, u32[]{:S(2)}) %collective-permute-start) | collective-permute-done | bytes 524320 | tf_op jit(solution)/shard_map/ppermute | solution.py:449
  46.1 0.1 collective-permute-done.1.refs_1_
  46.3 1.1 collective-permute-done.2.refs_2_
  47.3 0.0 all-gather.7.cloned.1.call-update
  47.4 0.0 all-gather.5.cloned.1.call-start
  47.4 1.7 collective-permute-start.12
  49.1 0.9 collective-permute-start.5
  50.1 2.2 %collective-permute-start.6 = (bf16[512,512]{1,0:T(8,128)(2,1)S(1)}, bf16[512,512]{1,0:T(8,128)(2,1)S(1)}, u32[]{:S(2)}, u32[]{:S(2)}) collective-permute-start(bf16[512,512]{1,0:T(8,128)(2,1)S(1)} %bitcast.13), channel_id=1, source_target_pairs={{0,18},{2,0},{16,2},{18,16},{1,19},{3,1},{17,3},{19,17},{4,22},{6,... | collective-permute-start | bytes 1572872 | tf_op jit(solution)/shard_map/ppermute | solution.py:449
  52.2 1.1 collective-permute-start.13
  53.4 0.0 collective-permute-start.11
  53.4 5.6 %collective-permute-done.12.refs_5_ = bf16[512,512]{1,0:T(8,128)(2,1)S(1)} collective-permute-done((bf16[512,512]{1,0:T(8,128)(2,1)S(1)}, bf16[512,512]{1,0:T(8,128)(2,1)S(1)}, u32[]{:S(2)}, u32[]{:S(2)}) %collective-permute-start.12) | collective-permute-done | bytes 524320 | tf_op jit(solution)/shard_map/ppermute | solution.py:449
  59.0 3.1 %collective-permute-start.14 = (bf16[512,512]{1,0:T(8,128)(2,1)S(1)}, bf16[512,512]{1,0:T(8,128)(2,1)S(1)}, u32[]{:S(2)}, u32[]{:S(2)}) collective-permute-start(bf16[512,512]{1,0:T(8,128)(2,1)S(1)} %collective-permute-done.12.refs_5_), channel_id=1, source_target_pairs={{0,12},{4,0},{8,4},{12,8},{1,13},{5,1},{9,5},{13,9},{2,14},{6,2},{... | collective-permute-start | bytes 1572872 | tf_op jit(solution)/shard_map/ppermute | solution.py:449
  62.1 0.5 collective-permute-done.5
  62.6 0.8 constant_dynamic-update-slice_fusion.1
  63.4 0.8 constant_dynamic-update-slice_fusion.refs_3_
  64.3 1.4 collective-permute-start.7
  65.6 2.4 %collective-permute-start.15 = (bf16[8,64,1024]{2,1,0:T(8,128)(2,1)}, bf16[8,64,1024]{2,1,0:T(8,128)(2,1)}, u32[]{:S(2)}, u32[]{:S(2)}) collective-permute-start(bf16[8,64,1024]{2,1,0:T(8,128)(2,1)} %all-to-all-done), channel_id=1, source_target_pairs={{0,16},{16,0},{1,17},{17,1},{2,18},{18,2},{3,19},{19,3},{4,20},{20... | collective-permute-start | bytes 3145736 | tf_op jit(solution)/shard_map/ppermute | solution.py:449
  68.0 0.5 collective-permute-start.4
  68.5 7.7 %collective-permute-done.11.refs_3_ = bf16[512,512]{1,0:T(8,128)(2,1)S(1)} collective-permute-done((bf16[512,512]{1,0:T(8,128)(2,1)S(1)}, bf16[512,512]{1,0:T(8,128)(2,1)S(1)}, u32[]{:S(2)}, u32[]{:S(2)}) %collective-permute-start.11) | collective-permute-done | bytes 524320 | tf_op jit(solution)/shard_map/ppermute | solution.py:449
  76.2 2.6 %lead_gram.1 = (f32[512,512]{1,0:T(8,128)S(1)}, bf16[8,512,512]{2,1,0:T(8,128)(2,1)S(1)}) custom-call(bf16[512,512]{1,0:T(8,128)(2,1)S(1)} %copy-done, bf16[512,512]{1,0:T(8,128)(2,1)S(1)} %collective-permute-done.1.refs_1_, bf16[512,512]{1,0:T(8,128)(2,1)S(1)} %collective-permute-done.2.refs_2_, bf16[512,512]{1,0:T(8,128)(2,1)S(1)} %collective-permute-done.11.refs_3_, ...), custom_call_target="tpu_custom_call" | custom-call | flops 4294967296 | bytes 65536 | tf_op jit(solution)/shard_map/lead_gram/pallas_call | solution.py:117
  78.9 2.0 %copy-done.1 = bf16[8,512,512]{2,1,0:T(8,128)(2,1)} copy-done((bf16[8,512,512]{2,1,0:T(8,128)(2,1)}, bf16[8,512,512]{2,1,0:T(8,128)(2,1)S(1)}, u32[]{:S(2)}) %copy-start.1) | copy-done | bytes 4194328
  80.9 5.3 %collective-permute-start.16 = (f32[512,512]{1,0:T(8,128)S(1)}, f32[512,512]{1,0:T(8,128)S(1)}, u32[]{:S(2)}, u32[]{:S(2)}) collective-permute-start(f32[512,512]{1,0:T(8,128)S(1)} %get-tuple-element.40.g0), channel_id=1, source_target_pairs={{0,1},{1,0},{2,3},{3,2},{4,5},{5,4},{6,7},{7,6},{8,9},{9,8},{10,11... | collective-permute-start | bytes 3145736 | tf_op jit(solution)/shard_map/ppermute | solution.py:449
  86.2 0.7 slice.3
  86.9 6.4 %collective-permute-done.7.refs_4_ = bf16[1024,512]{1,0:T(8,128)(2,1)} collective-permute-done((bf16[1024,512]{1,0:T(8,128)(2,1)}, bf16[1024,512]{1,0:T(8,128)(2,1)}, u32[]{:S(2)}, u32[]{:S(2)}) %collective-permute-start.7) | collective-permute-done | bytes 1048608 | tf_op jit(solution)/shard_map/ppermute | solution.py:449
  93.4 3.4 %collective-permute-start.3 = (bf16[1024,512]{1,0:T(8,128)(2,1)}, bf16[1024,512]{1,0:T(8,128)(2,1)}, u32[]{:S(2)}, u32[]{:S(2)}) collective-permute-start(bf16[1024,512]{1,0:T(8,128)(2,1)} %bitcast.refs_0_), channel_id=1, source_target_pairs={{0,12},{4,0},{8,4},{12,8},{1,13},{5,1},{9,5},{13,9},{2,14},{6,2},{... | collective-permute-start | bytes 3145736 | tf_op jit(solution)/shard_map/ppermute | solution.py:449
  96.8 1.9 collective-permute-done.4.refs_2_
  98.7 1.5 collective-permute-start.9
  100.2 11.3 %chol_first.1 = (f32[512,512]{1,0:T(8,128)S(1)}, f32[512,512]{1,0:T(8,128)S(1)}) custom-call(f32[512,512]{1,0:T(8,128)S(1)} %get-tuple-element.40.g0, f32[512,512]{1,0:T(8,128)S(1)} %collective-permute-done.16.g1, f32[1,512]{1,0:T(1,128)S(1)} %bitcast.8), custom_call_target="tpu_custom_call" | custom-call | flops 85899345920 | bytes 65536 | tf_op jit(solution)/shard_map/chol_first/pallas_call | solution.py:196
  111.5 10.8 %chol_second.1.refs_8_.inv_ref = f32[512,512]{1,0:T(8,128)S(1)} custom-call(f32[512,512]{1,0:T(8,128)S(1)} %get-tuple-element.41.a0, f32[512,512]{1,0:T(8,128)S(1)} %get-tuple-element.42.i0), custom_call_target="tpu_custom_call" | custom-call | flops 85899345920 | bytes 65536 | tf_op jit(solution)/shard_map/chol_second/pallas_call | solution.py:208
  122.4 0.0 all-gather.7.cloned.1.call-done
  122.4 16.8 %gram_first.1 = (f32[1024,512]{1,0:T(8,128)S(1)}, f32[1024,512]{1,0:T(8,128)}, f32[1024,512]{1,0:T(8,128)}, f32[512,512]{1,0:T(8,128)S(1)}, f32[512,512]{1,0:T(8,128)S(1)}, /*index=5*/bf16[2,256,1024]{2,1,0:T(8,128)(2,1)S(1)}) custom-call(bf16[1024,512]{1,0:T(8,128)(2,1)} %bitcast.refs_0_, bf16[1024,512]{1,0:T(8,128)(2,1)} %collective-permute-done.3.refs_1_, ...), custom_call_target="tpu_custom_call" | custom-call | flops 18253611008 | bytes 65536 | tf_op jit(solution)/shard_map/gram_first/pallas_call | solution.py:333
  139.2 1.3 copy-done.5
  140.5 1.0 copy-done.11
  141.5 2.1 %collective-permute-done.9.refs_6_.a0 = bf16[1024,512]{1,0:T(8,128)(2,1)} collective-permute-done((bf16[1024,512]{1,0:T(8,128)(2,1)}, bf16[1024,512]{1,0:T(8,128)(2,1)}, u32[]{:S(2)}, u32[]{:S(2)}) %collective-permute-start.9) | collective-permute-done | bytes 1048608 | tf_op jit(solution)/shard_map/ppermute | solution.py:449
  143.6 1.6 copy-done.3
  145.2 3.6 %gram_middle.1.rm = f32[1024,512]{1,0:T(8,128)S(1)} custom-call(bf16[1024,512]{1,0:T(8,128)(2,1)} %collective-permute-done.9.refs_6_.a0, bf16[1024,512]{1,0:T(8,128)(2,1)} %collective-permute-done.10.refs_7_.a1, bf16[8,512,512]{2,1,0:T(8,128)(2,1)S(1)} %copy-done.2, f32[1024,512]{1,0:T(8,128)S(1)} %copy-done.3), custom_call_target="tpu_custom_call" | custom-call | flops 5368709120 | bytes 65536 | tf_op jit(solution)/shard_map/gram_middle/pallas_call | solution.py:347
  148.8 4.8 %collective-permute-start.18 = (f32[1024,512]{1,0:T(8,128)S(1)}, f32[1024,512]{1,0:T(8,128)}, u32[]{:S(2)}, u32[]{:S(2)}) collective-permute-start(f32[1024,512]{1,0:T(8,128)S(1)} %gram_middle.1.rm), channel_id=1, source_target_pairs={{0,1},{1,0},{2,3},{3,2},{4,5},{5,4},{6,7},{7,6},{8,9},{9,8},{10,11... | collective-permute-start | bytes 6291464 | tf_op jit(solution)/shard_map/ppermute | solution.py:449
  153.6 16.1 %gram_second.1 = (f32[1024,512]{1,0:T(8,128)}, f32[1024,512]{1,0:T(8,128)}, f32[512,512]{1,0:T(8,128)}, f32[512,512]{1,0:T(8,128)}) custom-call(bf16[1024,512]{1,0:T(8,128)(2,1)} %bitcast.refs_0_, bf16[1024,512]{1,0:T(8,128)(2,1)} %collective-permute-done.3.refs_1_, bf16[1024,512]{1,0:T(8,128)(2,1)} %collective-permute-done.4.refs_2_, ...), custom_call_target="tpu_custom_call" | custom-call | flops 10737418240 | bytes 65536 | tf_op jit(solution)/shard_map/gram_second/pallas_call | solution.py:360
  169.7 0.2 collective-permute-start.17
  169.9 0.4 collective-permute-start.19
  170.4 1.4 copy-done.7
  171.8 6.4 %panel.1.p_ref = f32[1024,512]{1,0:T(8,128)S(1)} custom-call(f32[1024,512]{1,0:T(8,128)S(1)} %gram_middle.1.rm, f32[1024,512]{1,0:T(8,128)} %collective-permute-done.18.rr, f32[512,512]{1,0:T(8,128)S(1)} %copy-done.7, f32[1,512]{1,0:T(1,128)S(1)} %bitcast.9), custom_call_target="tpu_custom_call" | custom-call | flops 5368709120 | bytes 65536 | tf_op jit(solution)/shard_map/panel/pallas_call | solution.py:397
  178.2 9.2 %final.1 = f32[1024,1,512]{2,1,0:T(1,128)} custom-call(f32[1024,512]{1,0:T(8,128)S(1)} %copy-done.4, f32[1024,512]{1,0:T(8,128)} %collective-permute-done.17.tr, f32[1024,512]{1,0:T(8,128)S(1)} %panel.1.p_ref, f32[512,512]{1,0:T(8,128)S(1)} %copy-done.9, f32[512,512]{1,0:T(8,128)S(1)} %collective-permute-done.19.lr, f32[512,512]{1,0:T(8,128)S(1)} %copy-done.8, ...), custom_call_target="tpu_custom_call" | custom-call | flops 9663676416 | bytes 65536 | tf_op jit(solution)/shard_map/final/pallas_call | solution.py:434
  (46 shorter events, 0.1 us)
Async XLA Ops:
  15.8 6.4 %copy-start = (bf16[512,512]{1,0:T(8,128)(2,1)S(1)}, bf16[512,512]{1,0:T(8,128)(2,1)}, u32[]{:S(2)}) copy-start(bf16[512,512]{1,0:T(8,128)(2,1)} %get-tuple-element.30.refs_0_) | copy-start | bytes 1572868
  15.8 33.3 %copy-start.15 = (bf16[8,64,512]{2,1,0:T(8,128)(2,1)S(1)}, bf16[8,64,512]{2,1,0:T(8,128)(2,1)}, u32[]{:S(2)}) copy-start(bf16[8,64,512]{2,1,0:T(8,128)(2,1)} %get-tuple-element.34) | copy-start | bytes 1572868
  15.9 34.2 %copy-start.14 = (bf16[8,64,512]{2,1,0:T(8,128)(2,1)S(1)}, bf16[8,64,512]{2,1,0:T(8,128)(2,1)}, u32[]{:S(2)}) copy-start(bf16[8,64,512]{2,1,0:T(8,128)(2,1)} %get-tuple-element.35) | copy-start | bytes 1572868
  15.9 31.5 %all-to-all-start = ((bf16[8,64,1024]{2,1,0:T(8,128)(2,1)}), bf16[8,64,1024]{2,1,0:T(8,128)(2,1)}, u32[]{:S(2)}, u32[]{:S(2)}) async-start(bf16[8,64,1024]{2,1,0:T(8,128)(2,1)} %get-tuple-element.31), calls=%async_computation | async-start | bytes 2097152 | tf_op jit(solution)/shard_map/all_to_all | solution.py:465
  22.2 100.2 %all-gather.7.cloned.1.call-start = ((), (), s32[]{:S(2)}) async-start(), calls=%async_computation.2 | async-start | bytes 5242880 | tf_op jit(solution)/shard_map/all_gather | solution.py:474
  22.3 23.9 %collective-permute-start = (bf16[512,512]{1,0:T(8,128)(2,1)S(1)}, bf16[512,512]{1,0:T(8,128)(2,1)S(1)}, u32[]{:S(2)}, u32[]{:S(2)}) collective-permute-start(bf16[512,512]{1,0:T(8,128)(2,1)S(1)} %copy-done), channel_id=1, source_target_pairs={{0,2},{2,0},{1,3},{3,1},{4,6},{6,4},{5,7},{7,5},{8,10},{10,8},{9,1... | collective-permute-start | bytes 1572872 | tf_op jit(solution)/shard_map/ppermute | solution.py:449
  23.8 22.5 %collective-permute-start.1 = (bf16[512,512]{1,0:T(8,128)(2,1)S(1)}, bf16[512,512]{1,0:T(8,128)(2,1)S(1)}, u32[]{:S(2)}, u32[]{:S(2)}) collective-permute-start(bf16[512,512]{1,0:T(8,128)(2,1)S(1)} %copy-done), channel_id=1, source_target_pairs={{0,12},{4,0},{8,4},{12,8},{1,13},{5,1},{9,5},{13,9},{2,14},{6,2},{... | collective-permute-start | bytes 1572872 | tf_op jit(solution)/shard_map/ppermute | solution.py:449
  26.2 21.2 %collective-permute-start.2 = (bf16[512,512]{1,0:T(8,128)(2,1)S(1)}, bf16[512,512]{1,0:T(8,128)(2,1)S(1)}, u32[]{:S(2)}, u32[]{:S(2)}) collective-permute-start(bf16[512,512]{1,0:T(8,128)(2,1)S(1)} %copy-done), channel_id=1, source_target_pairs={{0,4},{4,8},{8,12},{12,0},{1,5},{5,9},{9,13},{13,1},{2,6},{6,10},{... | collective-permute-start | bytes 1572872 | tf_op jit(solution)/shard_map/ppermute | solution.py:449
  47.4 106.2 %all-gather.5.cloned.1.call-start = ((), (), s32[]{:S(2)}) async-start(), calls=%async_computation.1 | async-start | bytes 5242880 | tf_op jit(solution)/shard_map/all_gather | solution.py:475
  47.4 11.6 %collective-permute-start.12 = (bf16[512,512]{1,0:T(8,128)(2,1)S(1)}, bf16[512,512]{1,0:T(8,128)(2,1)S(1)}, u32[]{:S(2)}, u32[]{:S(2)}) collective-permute-start(bf16[512,512]{1,0:T(8,128)(2,1)S(1)} %collective-permute-done.refs_4_), channel_id=1, source_target_pairs={{0,12},{4,0},{8,4},{12,8},{1,13},{5,1},{9,5},{13,9},{2,14},{6,2},{... | collective-permute-start | bytes 1572872 | tf_op jit(solution)/shard_map/ppermute | solution.py:449
  49.1 13.5 %collective-permute-start.5 = (bf16[512,512]{1,0:T(8,128)(2,1)S(1)}, bf16[512,512]{1,0:T(8,128)(2,1)S(1)}, u32[]{:S(2)}, u32[]{:S(2)}) collective-permute-start(bf16[512,512]{1,0:T(8,128)(2,1)S(1)} %bitcast.14), channel_id=1, source_target_pairs={{0,2},{2,16},{16,18},{18,0},{1,3},{3,17},{17,19},{19,1},{4,6},{6,2... | collective-permute-start | bytes 1572872 | tf_op jit(solution)/shard_map/ppermute | solution.py:449
  50.1 13.4 %collective-permute-start.6 = (bf16[512,512]{1,0:T(8,128)(2,1)S(1)}, bf16[512,512]{1,0:T(8,128)(2,1)S(1)}, u32[]{:S(2)}, u32[]{:S(2)}) collective-permute-start(bf16[512,512]{1,0:T(8,128)(2,1)S(1)} %bitcast.13), channel_id=1, source_target_pairs={{0,18},{2,0},{16,2},{18,16},{1,19},{3,1},{17,3},{19,17},{4,22},{6,... | collective-permute-start | bytes 1572872 | tf_op jit(solution)/shard_map/ppermute | solution.py:449
  52.2 15.8 %collective-permute-start.13 = (bf16[512,512]{1,0:T(8,128)(2,1)S(1)}, bf16[512,512]{1,0:T(8,128)(2,1)S(1)}, u32[]{:S(2)}, u32[]{:S(2)}) collective-permute-start(bf16[512,512]{1,0:T(8,128)(2,1)S(1)} %collective-permute-done.refs_4_), channel_id=1, source_target_pairs={{0,4},{4,8},{8,12},{12,0},{1,5},{5,9},{9,13},{13,1},{2,6},{6,10},{... | collective-permute-start | bytes 1572872 | tf_op jit(solution)/shard_map/ppermute | solution.py:449
  53.4 22.9 %collective-permute-start.11 = (bf16[512,512]{1,0:T(8,128)(2,1)S(1)}, bf16[512,512]{1,0:T(8,128)(2,1)S(1)}, u32[]{:S(2)}, u32[]{:S(2)}) collective-permute-start(bf16[512,512]{1,0:T(8,128)(2,1)S(1)} %collective-permute-done.2.refs_2_), channel_id=1, source_target_pairs={{0,4},{4,8},{8,12},{12,0},{1,5},{5,9},{9,13},{13,1},{2,6},{6,10},{... | collective-permute-start | bytes 1572872 | tf_op jit(solution)/shard_map/ppermute | solution.py:449
  59.0 17.2 %collective-permute-start.14 = (bf16[512,512]{1,0:T(8,128)(2,1)S(1)}, bf16[512,512]{1,0:T(8,128)(2,1)S(1)}, u32[]{:S(2)}, u32[]{:S(2)}) collective-permute-start(bf16[512,512]{1,0:T(8,128)(2,1)S(1)} %collective-permute-done.12.refs_5_), channel_id=1, source_target_pairs={{0,12},{4,0},{8,4},{12,8},{1,13},{5,1},{9,5},{13,9},{2,14},{6,2},{... | collective-permute-start | bytes 1572872 | tf_op jit(solution)/shard_map/ppermute | solution.py:449
  64.3 29.1 %collective-permute-start.7 = (bf16[1024,512]{1,0:T(8,128)(2,1)}, bf16[1024,512]{1,0:T(8,128)(2,1)}, u32[]{:S(2)}, u32[]{:S(2)}) collective-permute-start(bf16[1024,512]{1,0:T(8,128)(2,1)} %constant_dynamic-update-slice_fusion.refs_3_), channel_id=1, source_target_pairs={{0,12},{4,0},{8,4},{12,8},{1,13},{5,1},{9,5},{13,9},{2,14},{6,2},{... | collective-permute-start | bytes 3145736 | tf_op jit(solution)/shard_map/ppermute | solution.py:449
  65.6 33.1 %collective-permute-start.15 = (bf16[8,64,1024]{2,1,0:T(8,128)(2,1)}, bf16[8,64,1024]{2,1,0:T(8,128)(2,1)}, u32[]{:S(2)}, u32[]{:S(2)}) collective-permute-start(bf16[8,64,1024]{2,1,0:T(8,128)(2,1)} %all-to-all-done), channel_id=1, source_target_pairs={{0,16},{16,0},{1,17},{17,1},{2,18},{18,2},{3,19},{19,3},{4,20},{20... | collective-permute-start | bytes 3145736 | tf_op jit(solution)/shard_map/ppermute | solution.py:449
  68.0 30.7 %collective-permute-start.4 = (bf16[1024,512]{1,0:T(8,128)(2,1)}, bf16[1024,512]{1,0:T(8,128)(2,1)}, u32[]{:S(2)}, u32[]{:S(2)}) collective-permute-start(bf16[1024,512]{1,0:T(8,128)(2,1)} %bitcast.refs_0_), channel_id=1, source_target_pairs={{0,4},{4,8},{8,12},{12,0},{1,5},{5,9},{9,13},{13,1},{2,6},{6,10},{... | collective-permute-start | bytes 3145736 | tf_op jit(solution)/shard_map/ppermute | solution.py:449
  78.9 2.0 %copy-start.1 = (bf16[8,512,512]{2,1,0:T(8,128)(2,1)}, bf16[8,512,512]{2,1,0:T(8,128)(2,1)S(1)}, u32[]{:S(2)}) copy-start(bf16[8,512,512]{2,1,0:T(8,128)(2,1)S(1)} %get-tuple-element.38.refs_6_.refs_8_.l_ref) | copy-start | bytes 12582916
  80.9 19.3 %collective-permute-start.16 = (f32[512,512]{1,0:T(8,128)S(1)}, f32[512,512]{1,0:T(8,128)S(1)}, u32[]{:S(2)}, u32[]{:S(2)}) collective-permute-start(f32[512,512]{1,0:T(8,128)S(1)} %get-tuple-element.40.g0), channel_id=1, source_target_pairs={{0,1},{1,0},{2,3},{3,2},{4,5},{5,4},{6,7},{7,6},{8,9},{9,8},{10,11... | collective-permute-start | bytes 3145736 | tf_op jit(solution)/shard_map/ppermute | solution.py:449
  86.9 35.4 %collective-permute-start.8 = (bf16[1024,512]{1,0:T(8,128)(2,1)}, bf16[1024,512]{1,0:T(8,128)(2,1)}, u32[]{:S(2)}, u32[]{:S(2)}) collective-permute-start(bf16[1024,512]{1,0:T(8,128)(2,1)} %constant_dynamic-update-slice_fusion.refs_3_), channel_id=1, source_target_pairs={{0,4},{4,8},{8,12},{12,0},{1,5},{5,9},{9,13},{13,1},{2,6},{6,10},{... | collective-permute-start | bytes 3145736 | tf_op jit(solution)/shard_map/ppermute | solution.py:449
  93.4 29.0 %collective-permute-start.3 = (bf16[1024,512]{1,0:T(8,128)(2,1)}, bf16[1024,512]{1,0:T(8,128)(2,1)}, u32[]{:S(2)}, u32[]{:S(2)}) collective-permute-start(bf16[1024,512]{1,0:T(8,128)(2,1)} %bitcast.refs_0_), channel_id=1, source_target_pairs={{0,12},{4,0},{8,4},{12,8},{1,13},{5,1},{9,5},{13,9},{2,14},{6,2},{... | collective-permute-start | bytes 3145736 | tf_op jit(solution)/shard_map/ppermute | solution.py:449
  98.7 42.8 %collective-permute-start.10 = (bf16[1024,512]{1,0:T(8,128)(2,1)}, bf16[1024,512]{1,0:T(8,128)(2,1)}, u32[]{:S(2)}, u32[]{:S(2)}) collective-permute-start(bf16[1024,512]{1,0:T(8,128)(2,1)} %collective-permute-done.7.refs_4_), channel_id=1, source_target_pairs={{0,12},{4,0},{8,4},{12,8},{1,13},{5,1},{9,5},{13,9},{2,14},{6,2},{... | collective-permute-start | bytes 3145736 | tf_op jit(solution)/shard_map/ppermute | solution.py:449
  98.7 44.9 %collective-permute-start.9 = (bf16[1024,512]{1,0:T(8,128)(2,1)}, bf16[1024,512]{1,0:T(8,128)(2,1)}, u32[]{:S(2)}, u32[]{:S(2)}) collective-permute-start(bf16[1024,512]{1,0:T(8,128)(2,1)} %collective-permute-done.4.refs_2_), channel_id=1, source_target_pairs={{0,4},{4,8},{8,12},{12,0},{1,5},{5,9},{9,13},{13,1},{2,6},{6,10},{... | collective-permute-start | bytes 3145736 | tf_op jit(solution)/shard_map/ppermute | solution.py:449
  122.3 16.8 %copy-start.6 = (f32[512,512]{1,0:T(8,128)}, f32[512,512]{1,0:T(8,128)S(1)}, u32[]{:S(2)}) copy-start(f32[512,512]{1,0:T(8,128)S(1)} %chol_second.1.refs_8_.inv_ref) | copy-start | bytes 3145732
  122.4 21.2 %copy-start.2 = (bf16[8,512,512]{2,1,0:T(8,128)(2,1)S(1)}, bf16[8,512,512]{2,1,0:T(8,128)(2,1)}, u32[]{:S(2)}) copy-start(bf16[8,512,512]{2,1,0:T(8,128)(2,1)} %copy-done.1) | copy-start | bytes 12582916
  139.2 1.3 copy-start.5
  140.5 1.0 copy-start.11
  141.5 7.3 %copy-start.10 = (f32[512,512]{1,0:T(8,128)}, f32[512,512]{1,0:T(8,128)S(1)}, u32[]{:S(2)}) copy-start(f32[512,512]{1,0:T(8,128)S(1)} %get-tuple-element.46.refs_13_) | copy-start | bytes 3145732
  141.5 7.3 %copy-start.12 = (bf16[2,256,1024]{2,1,0:T(8,128)(2,1)}, bf16[2,256,1024]{2,1,0:T(8,128)(2,1)S(1)}, u32[]{:S(2)}) copy-start(bf16[2,256,1024]{2,1,0:T(8,128)(2,1)S(1)} %get-tuple-element.43.refs_10_) | copy-start | bytes 3145732
  143.6 1.6 copy-start.3
  148.8 21.6 %collective-permute-start.18 = (f32[1024,512]{1,0:T(8,128)S(1)}, f32[1024,512]{1,0:T(8,128)}, u32[]{:S(2)}, u32[]{:S(2)}) collective-permute-start(f32[1024,512]{1,0:T(8,128)S(1)} %gram_middle.1.rm), channel_id=1, source_target_pairs={{0,1},{1,0},{2,3},{3,2},{4,5},{5,4},{6,7},{7,6},{8,9},{9,8},{10,11... | collective-permute-start | bytes 6291464 | tf_op jit(solution)/shard_map/ppermute | solution.py:449
  153.6 16.7 %copy-start.13 = (f32[8192]{0:T(1024)S(1)}, f32[8192]{0:T(1024)}, u32[]{:S(2)}) copy-start(f32[8192]{0:T(1024)} %param.3) | copy-start | bytes 98308
  169.7 8.5 %collective-permute-start.17 = (f32[1024,512]{1,0:T(8,128)}, f32[1024,512]{1,0:T(8,128)}, u32[]{:S(2)}, u32[]{:S(2)}) collective-permute-start(f32[1024,512]{1,0:T(8,128)} %get-tuple-element.49), channel_id=1, source_target_pairs={{0,1},{1,0},{2,3},{3,2},{4,5},{5,4},{6,7},{7,6},{8,9},{9,8},{10,11... | collective-permute-start | bytes 6291464 | tf_op jit(solution)/shard_map/ppermute | solution.py:449
  169.9 8.3 %collective-permute-start.19 = (f32[512,512]{1,0:T(8,128)}, f32[512,512]{1,0:T(8,128)S(1)}, u32[]{:S(2)}, u32[]{:S(2)}) collective-permute-start(f32[512,512]{1,0:T(8,128)} %get-tuple-element.52), channel_id=1, source_target_pairs={{0,1},{1,0},{2,3},{3,2},{4,5},{5,4},{6,7},{7,6},{8,9},{9,8},{10,11... | collective-permute-start | bytes 3145736 | tf_op jit(solution)/shard_map/ppermute | solution.py:449
  170.4 7.8 %copy-start.4 = (f32[1024,512]{1,0:T(8,128)S(1)}, f32[1024,512]{1,0:T(8,128)}, u32[]{:S(2)}) copy-start(f32[1024,512]{1,0:T(8,128)} %get-tuple-element.48.tm) | copy-start | bytes 6291460
  170.4 1.4 copy-start.7
  171.7 6.4 %copy-start.8 = (f32[512,512]{1,0:T(8,128)S(1)}, f32[512,512]{1,0:T(8,128)}, u32[]{:S(2)}) copy-start(f32[512,512]{1,0:T(8,128)} %copy-done.6) | copy-start | bytes 3145732
  171.7 6.5 %copy-start.9 = (f32[512,512]{1,0:T(8,128)S(1)}, f32[512,512]{1,0:T(8,128)}, u32[]{:S(2)}) copy-start(f32[512,512]{1,0:T(8,128)} %get-tuple-element.51.lm) | copy-start | bytes 3145732
Sparse Core Ops, SparseCore 0:
  47.5 50.5 all-gather.6
  100.3 52.5 all-gather.4
